TPU v7x, 128 devices: a whole 4x4x4 slice. The times are simulated.
128 devices in a mesh: ctx: 16 (over y_lo, x, core), head: 8 (over y_hi, z).
Axes of the slice: x: 4, y: 4 (y_hi: 2, y_lo: 2; y = y_hi * 2 + y_lo), z: 4, core: 2. Of those that a mesh axis runs over, the one named last changes fastest.
Arguments:
- queries: bfloat16 [4096, 8192], P('ctx', 'head'), may hold values from -5 to 5
- keys: bfloat16 [4096, 1024], P('ctx', 'head'), may hold values from -5 to 5
- values: bfloat16 [4096, 1024], P('ctx', 'head'), may hold values from -5 to 5
- gate_logit: bfloat16 [4096, 8], P('ctx', 'head'), may hold values from -4 to 2
- out_grad: bfloat16 [4096, 8192], P('ctx', 'head'), may hold values from -5 to 5
- stretch_place: int32 [32], replicated, may hold values from 0 to 31, as said below
Outputs:
- query_grad: bfloat16 [4096, 8192], P('ctx', 'head')
- key_grad: bfloat16 [4096, 1024], P('ctx', 'head')
- value_grad: bfloat16 [4096, 1024], P('ctx', 'head')
- gate_grad: float32 [4096, 8], P('ctx', 'head')
Inputs may be any that keep to these rules, and one draw needn't show every extreme that they name: `stretch_place`: entries 2d and 2d + 1 are the spans stored on index d of ctx; they sum to 31, and every span appears once.
All inputs are finite; a program needn't handle non-finite values.
Results may differ from a plain program's by a relative error of at most 0.025.
Values may be sent and summed in bfloat16 or wider, within the bound.
A program may use at most 64 MiB of HBM per device.

v0:
```python
import jax
import jax.numpy as jnp
from jax import lax
from jax.sharding import PartitionSpec as P

DELAY = 256


NEG_FILL = -1e30


def stored_positions(stretch_place, total_rows, span_rows):
    offsets = jnp.arange(total_rows, dtype=jnp.int32) % span_rows
    span_ids = jnp.repeat(stretch_place, span_rows, total_repeat_length=total_rows)
    return span_ids * span_rows + offsets


def block_scores(query_heads, key_block, gate_block, query_pos, key_pos):
    score_scale = key_block.shape[-1] ** (-0.5)
    scores = (
        jnp.einsum("qkgd,tkd->kgqt", query_heads, key_block, preferred_element_type=jnp.float32)
        * score_scale
    )
    offset = query_pos[:, None] - key_pos[None, :]
    evict_bias = jax.nn.log_sigmoid(-gate_block.astype(jnp.float32)).T
    delayed = (offset >= DELAY)[None, None]
    scores = scores + jnp.where(delayed, evict_bias[:, None, None, :], 0.0)
    live_mask = (offset >= 0)[None, None]
    return (jnp.where(live_mask, scores, NEG_FILL), live_mask, delayed)


def split_piece(key_piece, key_pos, span_rows):
    key_part, value_part, gate_part = key_piece
    piece_rows = key_part.shape[0]
    blocks = piece_rows // span_rows
    kv_heads = gate_part.shape[1]
    return (
        key_part.reshape(blocks, span_rows, kv_heads, -1),
        value_part.reshape(blocks, span_rows, kv_heads, -1),
        gate_part.reshape(blocks, span_rows, kv_heads),
        key_pos.reshape(blocks, span_rows),
    )


def forward_piece(softmax_state, key_piece, key_pos, query_heads, query_pos, span_rows):
    blocks_in = split_piece(key_piece, key_pos, span_rows)

    def update(running_in, key_block, value_block, gate_block, block_pos):
        run_max, run_total, run_acc = running_in
        scores, live_mask, delayed = block_scores(
            query_heads, key_block, gate_block, query_pos, block_pos
        )
        new_max = jnp.maximum(run_max, jnp.max(scores, axis=-1))
        factor = jnp.exp(run_max - new_max)
        weights = jnp.exp(scores - new_max[..., None])
        run_total = run_total * factor + jnp.sum(weights, axis=-1)
        run_acc = run_acc * factor[..., None] + jnp.einsum(
            "kgqt,tkd->kgqd", weights, value_block, preferred_element_type=jnp.float32
        )
        return (new_max, run_total, run_acc)

    def forward_per_block(running_in, block_in):
        key_block, value_block, gate_block, block_pos = block_in
        running_out = update(running_in, key_block, value_block, gate_block, block_pos)
        return (running_out, None)

    softmax_state, _ = lax.scan(forward_per_block, softmax_state, blocks_in)
    return softmax_state


def backward_piece(
    query_acc,
    key_piece,
    key_pos,
    query_heads,
    grad_heads,
    query_pos,
    log_total,
    delta_row,
    span_rows,
):
    blocks_in = split_piece(key_piece, key_pos, span_rows)
    piece_rows = key_piece[0].shape[0]
    kv_heads = key_piece[2].shape[1]
    head_size = query_heads.shape[-1]
    score_scale = head_size ** (-0.5)

    def terms(acc_in, key_block, value_block, gate_block, block_pos):
        scores, live_mask, delayed = block_scores(
            query_heads, key_block, gate_block, query_pos, block_pos
        )
        attn_prob = jnp.where(live_mask, jnp.exp(scores - log_total[..., None]), 0.0)
        prob_grad = jnp.einsum(
            "qkgd,tkd->kgqt", grad_heads, value_block, preferred_element_type=jnp.float32
        )
        score_grad = attn_prob * (prob_grad - delta_row[..., None])
        grad_low = score_grad.astype(jnp.bfloat16)
        prob_low = attn_prob.astype(jnp.bfloat16)
        acc_out = acc_in + jnp.einsum(
            "kgqt,tkd->qkgd", grad_low, key_block, preferred_element_type=jnp.float32
        )
        key_term = (
            jnp.einsum("kgqt,qkgd->tkd", grad_low, query_heads, preferred_element_type=jnp.float32)
            * score_scale
        )
        value_term = jnp.einsum(
            "kgqt,qkgd->tkd", prob_low, grad_heads, preferred_element_type=jnp.float32
        )
        gate_term = jnp.sum(jnp.where(delayed, score_grad, 0.0), axis=(1, 2)).T
        return (acc_out, (key_term, value_term, gate_term))

    def backward_per_block(acc_in, block_in):
        key_block, value_block, gate_block, block_pos = block_in
        return terms(acc_in, key_block, value_block, gate_block, block_pos)

    query_acc, stacked = lax.scan(backward_per_block, query_acc, blocks_in)
    key_terms = stacked[0].reshape(piece_rows, kv_heads * head_size)
    value_terms = stacked[1].reshape(piece_rows, kv_heads * head_size)
    gate_terms = stacked[2].reshape(piece_rows, kv_heads)
    return (query_acc, (key_terms, value_terms, gate_terms))


def softmax_totals(softmax_state, grad_heads):
    run_max, run_total, run_acc = softmax_state
    log_total = run_max + jnp.log(run_total)
    output = run_acc / run_total[..., None]
    delta_row = jnp.sum(grad_heads.astype(jnp.float32).transpose(1, 2, 0, 3) * output, axis=-1)
    return (log_total, delta_row)


def on_device(queries, keys, values, gate_logit, out_grad, stretch_place):
    tok_rows = queries.shape[0]
    span_rows = tok_rows // 2
    kv_heads = gate_logit.shape[1]
    head_size = keys.shape[1] // kv_heads
    group_size = queries.shape[1] // keys.shape[1]
    ctx_count = lax.axis_size("ctx")
    total_rows = tok_rows * ctx_count
    positions = stored_positions(stretch_place, total_rows, span_rows)
    my_index = lax.axis_index("ctx")
    query_pos = lax.dynamic_slice_in_dim(positions, my_index * tok_rows, tok_rows)
    query_heads = queries.reshape(tok_rows, kv_heads, group_size, head_size)
    grad_heads = out_grad.reshape(tok_rows, kv_heads, group_size, head_size)
    start_state = (
        jnp.full((kv_heads, group_size, tok_rows), NEG_FILL, jnp.float32),
        jnp.zeros((kv_heads, group_size, tok_rows), jnp.float32),
        jnp.zeros((kv_heads, group_size, tok_rows, head_size), jnp.float32),
    )
    start_query = jnp.zeros((tok_rows, kv_heads, group_size, head_size), jnp.float32)
    key_piece = (
        lax.all_gather(keys, "ctx", axis=0, tiled=True),
        lax.all_gather(values, "ctx", axis=0, tiled=True),
        lax.all_gather(gate_logit, "ctx", axis=0, tiled=True),
    )
    key_pos = lax.slice_in_dim(positions, 0, key_piece[0].shape[0], axis=0)
    softmax_state = forward_piece(
        start_state, key_piece, key_pos, query_heads, query_pos, span_rows
    )
    log_total, delta_row = softmax_totals(softmax_state, grad_heads)
    key_piece = (
        lax.all_gather(keys, "ctx", axis=0, tiled=True),
        lax.all_gather(values, "ctx", axis=0, tiled=True),
        lax.all_gather(gate_logit, "ctx", axis=0, tiled=True),
    )
    row_start = jnp.int32(0)
    query_acc = start_query
    key_all = jnp.zeros((total_rows, kv_heads * head_size), jnp.float32)
    value_all = jnp.zeros((total_rows, kv_heads * head_size), jnp.float32)
    gate_all = jnp.zeros((total_rows, kv_heads), jnp.float32)
    piece_rows = key_piece[0].shape[0]
    key_pos = lax.dynamic_slice_in_dim(positions, row_start, piece_rows)
    query_acc, piece_terms = backward_piece(
        query_acc,
        key_piece,
        key_pos,
        query_heads,
        grad_heads,
        query_pos,
        log_total,
        delta_row,
        span_rows,
    )
    key_all = lax.dynamic_update_slice_in_dim(key_all, key_all + piece_terms[0], row_start, 0)
    value_all = lax.dynamic_update_slice_in_dim(value_all, value_all + piece_terms[1], row_start, 0)
    gate_all = lax.dynamic_update_slice_in_dim(gate_all, gate_all + piece_terms[2], row_start, 0)
    query_acc, key_all, value_all, gate_all = (query_acc, key_all, value_all, gate_all)
    key_sum, value_sum, gate_sum = (
        lax.psum_scatter(key_all, "ctx", scatter_dimension=0, tiled=True),
        lax.psum_scatter(value_all, "ctx", scatter_dimension=0, tiled=True),
        lax.psum_scatter(gate_all, "ctx", scatter_dimension=0, tiled=True),
    )
    keep_prob = jax.nn.sigmoid(gate_logit.astype(jnp.float32))
    score_scale = head_size ** (-0.5)
    query_grad = (
        (query_acc * score_scale)
        .reshape(tok_rows, kv_heads * group_size * head_size)
        .astype(jnp.bfloat16)
    )
    return (
        query_grad,
        key_sum.astype(jnp.bfloat16),
        value_sum.astype(jnp.bfloat16),
        -keep_prob * gate_sum,
    )


def solution(mesh):
    in_specs = (
        P("ctx", "head"),
        P("ctx", "head"),
        P("ctx", "head"),
        P("ctx", "head"),
        P("ctx", "head"),
        P(),
    )
    out_specs = (P("ctx", "head"), P("ctx", "head"), P("ctx", "head"), P("ctx", "head"))
    return jax.shard_map(
        on_device, mesh=mesh, in_specs=in_specs, out_specs=out_specs, check_vma=False
    )
```

profile of v0, /device:TPU:0, one launch (start us, length us, event | category | flops | bytes accessed | tf_op | source)
XLA Modules:
  0.0 570.1 jit_solution(8219516724253999199)
XLA Ops:
  8.8 1.3 copy.27
  10.3 2.0 copy.29
  12.4 1.3 copy.32
  13.7 19.8 %all_gather.13 = bf16[4096,1]{0,1:T(2,128)(2,1)S(1)} all-gather(bf16[256,1]{0,1:T(2,128)(2,1)S(1)} %copy-done.1), channel_id=1, replica_groups=mesh['ctx'=16,'head'=8] {'ctx'}, dimensions={0}, use_global_device_ids=true | all-gather | bytes 8704 | tf_op jit(solution)/shard_map/all_gather | solution.py:163
  35.0 4.4 compare_select_fusion.3
  40.6 15.7 %fusion.58 = (s32[32,128]{1,0:T(8,128)S(1)}, s32[4096]{0:T(1024)S(1)}) fusion(pred[4096]{0:T(1024)(128)(4,1)S(1)} %get-tuple-element.302, pred[4096]{0:T(1024)(128)(4,1)S(1)} %get-tuple-element.301, pred[4096]{0:T(1024)(128)(4,1)S(1)} %get-tuple-element.300, pred[4096]{0:T(1024)(128)(4,1)S(1)} %get-tuple-element.299, ...), kind=kLoop, calls=%fused_computation.121 | loop fusion | flops 163840 | bytes 151652 | tf_op jit(solution)/shard_map/add | solution.py:15
  56.4 22.4 %all-gather.5.cloned.1.call-done = bf16[4096,128]{1,0:T(8,128)(2,1)} async-done(((bf16[256,128]{1,0:T(8,128)(2,1)}), bf16[4096,128]{1,0:T(8,128)(2,1)}) %all-gather.5.cloned.1.call-update) | async-done | bytes 1048592 | tf_op jit(solution)/shard_map/all_gather | solution.py:162
  78.8 103.9 %while.33 = (s32[]{:T(128)}, f32[1,8,256]{2,1,0:T(8,128)S(1)}, f32[1,8,256]{2,1,0:T(8,128)S(1)}, f32[1,8,256,128]{3,2,1,0:T(8,128)S(1)}, s32[256]{0:T(256)S(1)},...) while((s32[]{:T(128)}, f32[1,8,256]{2,1,0:T(8,128)S(1)}, ...), condition=%wide.region_3.4_spmd.clone, body=%wide.region_0.3_spmd.clone.sunk | while | flops 137016320 | bytes 6296985 | solution.py:67
  80.4 1.6 fusion.99
  83.6 1.6 fusion.99
  86.8 1.6 fusion.99
  90.1 1.6 fusion.99
  93.3 1.6 fusion.99
  96.6 1.6 fusion.99
  99.8 1.6 fusion.99
  103.1 1.6 fusion.99
  106.3 1.6 fusion.99
  109.6 1.6 fusion.99
  112.8 1.6 fusion.99
  116.1 1.6 fusion.99
  119.3 1.6 fusion.99
  122.6 1.6 fusion.99
  125.8 1.6 fusion.99
  129.1 1.6 fusion.99
  132.3 1.6 fusion.99
  135.6 1.6 fusion.99
  138.8 1.6 fusion.99
  142.1 1.6 fusion.99
  145.3 1.6 fusion.99
  148.5 1.6 fusion.99
  151.8 1.6 fusion.99
  155.0 1.6 fusion.99
  158.3 1.6 fusion.99
  161.5 1.6 fusion.99
  164.8 1.6 fusion.99
  168.0 1.6 fusion.99
  171.3 1.6 fusion.99
  174.5 1.6 fusion.99
  177.8 1.6 fusion.99
  181.0 1.6 fusion.99
  182.7 1.3 copy.30
  184.1 1.6 fusion.56
  185.6 182.6 %while.34 = (s32[]{:T(128)}, f32[256,1,8,128]{0,3,2,1:T(8,128)S(1)}, f32[32,128,1,128]{3,1,2,0:T(8,128)}, f32[32,128,1,128]{3,1,2,0:T(8,128)}, f32[32,128,1]{1,2...) while((s32[]{:T(128)}, ...), condition=%wide.region_7.8_spmd.clone, body=%wide.region_5.7_spmd.clone.sunk | while | flops 339166080 | bytes 9558983 | solution.py:116
  188.3 1.2 fusion.111
  194.0 1.2 fusion.111
  216.8 1.2 fusion.111
  222.5 1.2 fusion.111
  228.2 1.2 fusion.111
  239.6 1.2 fusion.111
  245.3 1.2 fusion.111
  256.8 1.2 fusion.111
  273.9 1.2 fusion.111
  291.0 1.2 fusion.111
  296.7 1.2 fusion.111
  319.5 1.2 fusion.111
  325.2 1.2 fusion.111
  353.7 1.2 fusion.111
  359.4 1.2 fusion.111
  368.2 2.0 copy.39
  372.5 61.3 %reduce-scatter.10.cloned.1.call-done = f32[256,1]{1,0:T(8,128)} async-done(((f32[4096,1]{1,0:T(8,128)}), f32[256,1]{1,0:T(8,128)}) %reduce-scatter.10.cloned.1.call-update) | async-done | bytes 1040
  435.3 62.6 %reduce-scatter.6.cloned.1.call-done = f32[256,128]{1,0:T(8,128)} async-done(((f32[4096,128]{1,0:T(8,128)}), f32[256,128]{1,0:T(8,128)}) %reduce-scatter.6.cloned.1.call-update) | async-done | bytes 131088 | tf_op jit(solution)/shard_map/reduce_scatter | solution.py:188
  497.9 1.5 convert_element_type.56
  499.4 62.6 %reduce-scatter.8.cloned.1.call-done = f32[256,128]{1,0:T(8,128)} async-done(((f32[4096,128]{1,0:T(8,128)}), f32[256,128]{1,0:T(8,128)}) %reduce-scatter.8.cloned.1.call-update) | async-done | bytes 131088 | tf_op jit(solution)/shard_map/reduce_scatter | solution.py:189
  562.1 1.5 convert_element_type.57
  (629 shorter events, 219.7 us)
Async XLA Ops:
  7.2 49.3 %all-gather.3.cloned.1.call-start = ((), (), s32[]{:S(2)}) async-start(), calls=%async_computation.3 | async-start | bytes 1114112 | tf_op jit(solution)/shard_map/all_gather | solution.py:161
  7.9 70.9 %all-gather.5.cloned.1.call-start = ((), (), s32[]{:S(2)}) async-start(), calls=%async_computation.4 | async-start | bytes 1114112 | tf_op jit(solution)/shard_map/all_gather | solution.py:162
  8.6 425.1 %reduce-scatter.10.cloned.1.call-start = ((), (), s32[]{:S(2)}) async-start(), calls=%async_computation.7 | async-start | bytes 2228224
  8.8 4.9 copy-start.1
  8.8 24.7 %copy-start = (s32[32]{0:T(128)S(1)}, s32[32]{0:T(128)}, u32[]{:S(2)}) copy-start(s32[32]{0:T(128)} %param.17) | copy-start | bytes 388
  370.2 127.7 %reduce-scatter.6.cloned.1.call-start = ((), (), s32[]{:S(2)}) async-start(), calls=%async_computation.5 | async-start | bytes 2228224 | tf_op jit(solution)/shard_map/reduce_scatter | solution.py:188
  370.8 191.3 %reduce-scatter.8.cloned.1.call-start = ((), (), s32[]{:S(2)}) async-start(), calls=%async_computation.6 | async-start | bytes 2228224 | tf_op jit(solution)/shard_map/reduce_scatter | solution.py:189
Sparse Core Ops, SparseCore 0:
  9.7 34.8 all-gather.2
  46.3 32.4 all-gather.4
  370.3 63.3 reduce-scatter.9
  436.0 61.8 reduce-scatter.5
  500.1 61.8 reduce-scatter.7
where the time goes:
time: 582 us; the launch traced here: 570 us
  matrix products  262 us (45%)
  waiting for transfers between devices  211 us (36%)
  other arithmetic  46.7 us (8%)
  blocking collectives  19.8 us (3%)
  between operations  13.9 us (2%)
  local copies, waits for them, and re-layouts  12.6 us (2%)
    dot_general x64, matrix products, block_scores(): jnp.einsum('qkgd,tkd->kgqt', query_heads, key_block, preferred_element_ty...  74 us
    unnamed x6, waiting for transfers between devices  63.7 us
    reduce_scatter x1, waiting for transfers between devices, on_device(): lax.psum_scatter(value_all, 'ctx', scatter_dimension=0, tiled=True)  62.6 us
    reduce_scatter x1, waiting for transfers between devices, on_device(): lax.psum_scatter(key_all, 'ctx', scatter_dimension=0, tiled=True)  62.6 us
    dot_general x32, matrix products, update(): jnp.einsum('kgqt,tkd->kgqd', weights, value_block, preferred_element_type...  52.8 us
    dot_general x32, matrix products, terms(): jnp.einsum('kgqt,tkd->qkgd', grad_low, key_block, preferred_element_type=...  39.1 us
    dot_general x32, matrix products, terms(): jnp.einsum('qkgd,tkd->kgqt', grad_heads, value_block, preferred_element_t...  37.6 us
    dot_general x32, matrix products, terms(): jnp.einsum('kgqt,qkgd->tkd', prob_low, grad_heads, preferred_element_type...  29.1 us
  transfers between devices with their start and end apart: 5, of which 4 were waited for; matrix products, arithmetic and copies ran while one was open for 6% of the time, Pallas kernels for 0%

commit v1 on v0

v1 whole, which is shorter than its diff:
```python
import functools

import jax
import jax.numpy as jnp
from jax import lax
from jax.experimental import pallas as pl
from jax.experimental.pallas import tpu as pltpu
from jax.sharding import PartitionSpec as P

DELAY = 256
SPAN = 128
HEADS = 8
WIDE = SPAN * HEADS
CHIPS = 8
STEPS = 17
ROWS = 528
NEG = -1e30
LOG2E = 1.4426950408889634
SCALE = 128 ** (-0.5)
MESH = pl.DeviceIdType.MESH
F32, BF16 = jnp.float32, jnp.bfloat16


def step_slot(s):
    half, odd = lax.div(s, 2), lax.rem(s, 2)
    first = lax.div(1, half + 1)
    return 2 * half - odd - lax.div(s, 16) + first * odd


def forward_step(i):
    half, odd = lax.div(i, 2), lax.rem(i, 2)
    second = lax.div(2, half + 1) - 2 * lax.div(1, half + 1)
    return i + second * (1 - 2 * odd)


def chip_at(y, x, j, sign):
    dy, dx = lax.div(j, 4), lax.rem(j, 4)
    return lax.rem(y + 2 + sign * dy, 2) * 4 + lax.rem(x + 4 + sign * dx, 4)


def kernel(
    place, q_ref, k_ref, v_ref, gate_ref, o_ref,
    dq_ref, dk_ref, dv_ref, dg_ref,
    blocks, qc, qct, oc, oct_, wt_all, e_all, p_all, stat, total, ds_all,
    cur, cur_gate, own, own_gate, pre_out, pre_in, sum_out, sum_in,
    own_send, fwd_send, block_recv, pre_send, pre_recv, sum_send, sum_recv,
):
    me = lax.axis_index("ctx")
    core = lax.rem(me, 2)
    chip = lax.div(me, 2)
    y, x = lax.div(chip, 4), lax.rem(chip, 4)
    partner = me + 1 - 2 * core

    barrier = pltpu.get_barrier_semaphore()
    pl.semaphore_signal(barrier, inc=1, device_id={"ctx": partner}, device_id_type=MESH)
    for j in range(1, CHIPS):
        other = chip_at(y, x, jnp.int32(j), 1) * 2 + core
        pl.semaphore_signal(barrier, inc=1, device_id={"ctx": other}, device_id_type=MESH)

    blocks[0, 0:256, :] = k_ref[...]
    blocks[0, 256:512, :] = v_ref[...]
    blocks[0, 512:528, :] = gate_ref[...]
    pl.semaphore_wait(barrier, CHIPS)

    def own_copy(j):
        if j == 0:
            target, slot = partner, 1
        else:
            target, slot = chip_at(y, x, jnp.int32(j), 1) * 2 + core, 2 * j
        return pltpu.make_async_remote_copy(
            src_ref=blocks.at[0], dst_ref=blocks.at[slot], send_sem=own_send.at[j],
            recv_sem=block_recv.at[slot], device_id={"ctx": target}, device_id_type=MESH)

    def forward_copy(j):
        return pltpu.make_async_remote_copy(
            src_ref=blocks.at[2 * j], dst_ref=blocks.at[2 * j + 1], send_sem=fwd_send.at[j],
            recv_sem=block_recv.at[2 * j + 1], device_id={"ctx": partner}, device_id_type=MESH)

    def pre_copy(j):
        return pltpu.make_async_remote_copy(
            src_ref=pre_out.at[j], dst_ref=pre_in.at[j], send_sem=pre_send.at[j],
            recv_sem=pre_recv.at[j], device_id={"ctx": partner}, device_id_type=MESH)

    def sum_copy(j):
        target = chip_at(y, x, j, -1) * 2 + core
        return pltpu.make_async_remote_copy(
            src_ref=sum_out.at[j], dst_ref=sum_in.at[j], send_sem=sum_send.at[j],
            recv_sem=sum_recv.at[j], device_id={"ctx": target}, device_id_type=MESH)

    for j in range(CHIPS):
        own_copy(j).start()

    for h in range(HEADS):
        wide = slice(h * SPAN, (h + 1) * SPAN)
        for q in range(2):
            part = slice(q * SPAN, (q + 1) * SPAN)
            for src, plain, turned in ((q_ref, qc, qct), (o_ref, oc, oct_)):
                tile = src[part, wide]
                plain[wide, part] = tile
                turned[part, wide] = tile.T

    key_row = lax.broadcasted_iota(jnp.int32, (SPAN, SPAN), 0)
    query_col = lax.broadcasted_iota(jnp.int32, (SPAN, SPAN), 1)
    lag = query_col - key_row
    a0, a1 = place[2 * me], place[2 * me + 1]
    a_low = jnp.minimum(a0, a1)
    q_high = (a1 > a0).astype(jnp.int32)

    def pairs(s):
        slot = step_slot(s)
        theirs = chip_at(y, x, lax.div(slot, 2), -1) * 2 + lax.rem(core + slot, 2)
        b0, b1 = place[2 * theirs], place[2 * theirs + 1]
        k_low = (b1 < b0).astype(jnp.int32)
        below = jnp.minimum(b0, b1) < a_low
        diag = s == 0
        cross = s == 1
        k0 = jnp.where(diag, 0, jnp.where(cross, k_low, jnp.where(below, k_low, 0)))
        k1 = jnp.where(diag, 1, jnp.where(cross, k_low, jnp.where(below, k_low, 1)))
        q0 = jnp.where(diag, 0, jnp.where(cross, q_high, jnp.where(below, 0, q_high)))
        q1 = jnp.where(diag, 1, jnp.where(cross, q_high, jnp.where(below, 1, q_high)))
        out = []
        for u, (k, q) in enumerate(((k0, q0), (k1, q1))):
            apart = jnp.where(q == 0, a0, a1) - jnp.where(k == 0, b0, b1)
            live = -SPAN * apart
            if u == 1:
                live = jnp.where(cross, 4 * SPAN, live)
            out.append((k, q, DELAY - SPAN * apart, live))
        return slot, out

    def take(first, a, b):
        return lax.select(first, a, b)

    def first_pass(i, _):
        s = forward_step(i)
        slot, units = pairs(s)

        @pl.when(s >= 2)
        def _():
            pltpu.make_async_remote_copy(
                src_ref=blocks.at[slot], dst_ref=blocks.at[slot], send_sem=own_send.at[0],
                recv_sem=block_recv.at[slot], device_id={"ctx": partner}, device_id_type=MESH).wait_recv()

            @pl.when(lax.rem(slot, 2) == 0)
            def _():
                forward_copy(lax.div(slot, 2)).start()

        k0, k1 = blocks[slot, 0:128, :].astype(F32), blocks[slot, 128:256, :].astype(F32)
        v0, v1 = blocks[slot, 256:384, :].astype(F32), blocks[slot, 384:512, :].astype(F32)
        gates = blocks[slot, 512:528, :].astype(F32)
        evict = -LOG2E * (jnp.maximum(gates, 0.0) + jnp.log(1.0 + jnp.exp(-jnp.abs(gates))))
        zero = jnp.zeros((SPAN, SPAN), F32)
        wk, wv, bias = [], [], []
        for u, (k, q, least, live) in enumerate(units):
            ku, vu = take(k == 0, k0, k1), take(k == 0, v0, v1)
            wk.append(jnp.concatenate([take(q == 0, ku, zero), take(q == 0, zero, ku)], axis=1).astype(BF16))
            wv.append(jnp.concatenate([take(q == 0, vu, zero), take(q == 0, zero, vu)], axis=1).astype(BF16))
            kt = ku.T
            columns = pl.ds(pl.multiple_of(s * 256 + u * SPAN, SPAN), SPAN)
            wt_all[0:128, columns] = take(q == 0, kt, zero).astype(BF16)
            wt_all[128:256, columns] = take(q == 0, zero, kt).astype(BF16)
            column = jnp.broadcast_to(take(k == 0, evict[0:1, :], evict[1:2, :]), (SPAN, SPAN)).T
            bias.append(jnp.where(lag >= live, jnp.where(lag >= least, column, 0.0), NEG))
        wk, wv = jnp.concatenate(wk, axis=0), jnp.concatenate(wv, axis=0)
        for c in range(4):
            cols = slice(c * 256, (c + 1) * 256)
            scores = jnp.dot(wk, qct[:, cols], preferred_element_type=F32)
            grads = jnp.dot(wv, oct_[:, cols], preferred_element_type=F32)
            for u in range(2):
                part = slice(u * SPAN, (u + 1) * SPAN)
                for h in range(2):
                    lane = slice(h * SPAN, (h + 1) * SPAN)
                    wide = slice(c * 256 + h * SPAN, c * 256 + (h + 1) * SPAN)
                    score = scores[part, lane] * (SCALE * LOG2E) + bias[u]
                    grad = grads[part, lane]
                    top = jnp.max(score, axis=0, keepdims=True)
                    e = jnp.exp2(score - top)
                    e_all[s, part, wide] = e
                    p_all[s, part, wide] = grad
                    stat[s, u:u + 1, wide] = top
                    stat[s, 2 + u:3 + u, wide] = jnp.sum(e, axis=0, keepdims=True)
                    stat[s, 4 + u:5 + u, wide] = jnp.sum(e * grad, axis=0, keepdims=True)
        return 0

    lax.fori_loop(0, STEPS, first_pass, 0)

    row = lax.broadcasted_iota(jnp.int32, (2, 1), 0)

    def combine(s, carry):
        top, mass, weighted = carry
        _, units = pairs(s)
        new = top
        for u, (_, q, _, _) in enumerate(units):
            new = jnp.maximum(new, jnp.where(row == q, stat[s, u:u + 1, :], NEG))
        keep = jnp.exp2(top - new)
        mass, weighted = mass * keep, weighted * keep
        for u, (_, q, _, _) in enumerate(units):
            factor = jnp.exp2(jnp.minimum(stat[s, u:u + 1, :] - new, 0.0))
            mass = mass + jnp.where(row == q, stat[s, 2 + u:3 + u, :] * factor, 0.0)
            weighted = weighted + jnp.where(row == q, stat[s, 4 + u:5 + u, :] * factor, 0.0)
        return new, mass, weighted

    start = (jnp.full((2, WIDE), NEG, F32), jnp.zeros((2, WIDE), F32), jnp.zeros((2, WIDE), F32))
    top, mass, weighted = lax.fori_loop(0, STEPS, combine, start)
    total[0:2, :] = top
    total[2:4, :] = 1.0 / mass
    total[4:6, :] = weighted / mass

    def pack(dst, key_part, value_part, gate_part):
        dst[0:256, :] = key_part.astype(BF16)
        dst[256:512, :] = value_part.astype(BF16)
        high = gate_part.astype(BF16).astype(F32)
        dst[512:528, :] = jnp.concatenate([high, gate_part - high], axis=0).astype(BF16)

    def unpack(src):
        tail = src[512:528, :].astype(F32)
        return src[0:256, :].astype(F32), src[256:512, :].astype(F32), tail[0:8] + tail[8:16]

    def second_pass(i, _):
        s = STEPS - 1 - i
        slot, units = pairs(s)
        j = lax.div(slot, 2)
        scale_rows, delta_rows = [], []
        for u, (_, q, _, _) in enumerate(units):
            first = q == 0
            peak = take(first, total[0:1, :], total[1:2, :])
            inverse = take(first, total[2:3, :], total[3:4, :])
            scale_rows.append(jnp.exp2(stat[s, u:u + 1, :] - peak) * inverse)
            delta_rows.append(take(first, total[4:5, :], total[5:6, :]))
        value_acc = jnp.zeros((256, 256), F32)
        key_acc = jnp.zeros((256, 256), F32)
        gate_acc = [jnp.zeros((SPAN, SPAN), F32), jnp.zeros((SPAN, SPAN), F32)]
        for c in range(4):
            cols = slice(c * 256, (c + 1) * 256)
            prob_rows, grad_rows = [], []
            for u in range(2):
                part = slice(u * SPAN, (u + 1) * SPAN)
                prob = e_all[s, part, cols] * scale_rows[u][:, cols]
                grad = prob * (p_all[s, part, cols] - delta_rows[u][:, cols])
                gate_acc[u] = gate_acc[u] + grad[:, 0:128] + grad[:, 128:256]
                prob_rows.append(prob.astype(BF16))
                grad_rows.append(grad.astype(BF16))
            prob_low = jnp.concatenate(prob_rows, axis=0)
            grad_low = jnp.concatenate(grad_rows, axis=0)
            ds_all[pl.ds(pl.multiple_of(s * 256, 256), 256), cols] = grad_low
            value_acc = value_acc + jnp.dot(prob_low, oc[cols, :], preferred_element_type=F32)
            key_acc = key_acc + jnp.dot(grad_low, qc[cols, :], preferred_element_type=F32)
        zero = jnp.zeros((SPAN, SPAN), F32)
        key_out, value_out = [zero, zero], [zero, zero]
        gate_out = [jnp.zeros((1, SPAN), F32), jnp.zeros((1, SPAN), F32)]
        for u, (k, q, least, _) in enumerate(units):
            part = slice(u * SPAN, (u + 1) * SPAN)
            key_u = take(q == 0, key_acc[part, 0:128], key_acc[part, 128:256]) * SCALE
            value_u = take(q == 0, value_acc[part, 0:128], value_acc[part, 128:256])
            gate_u = jnp.sum(jnp.where(lag >= least, gate_acc[u], 0.0).T, axis=0, keepdims=True)
            for half in range(2):
                hit = k == half
                key_out[half] = key_out[half] + take(hit, key_u, zero)
                value_out[half] = value_out[half] + take(hit, value_u, zero)
                gate_out[half] = gate_out[half] + take(hit, gate_u, jnp.zeros((1, SPAN), F32))
        cur[0:128, :] = key_out[0]
        cur[128:256, :] = key_out[1]
        cur[256:384, :] = value_out[0]
        cur[384:512, :] = value_out[1]
        cur_gate[...] = jnp.concatenate(gate_out + [jnp.zeros((6, SPAN), F32)], axis=0)

        @pl.when(lax.rem(slot, 2) == 1)
        def _():
            pack(pre_out.at[j], cur[0:256, :], cur[256:512, :], cur_gate[...])
            pre_copy(j).start()

        @pl.when(jnp.logical_and(lax.rem(slot, 2) == 0, s >= 2))
        def _():
            pre_copy(j).wait_recv()
            more = unpack(pre_in.at[j])
            pack(sum_out.at[j], cur[0:256, :] + more[0], cur[256:512, :] + more[1], cur_gate[...] + more[2])
            sum_copy(j).start()

        @pl.when(s == 1)
        def _():
            own[...] = cur[...]
            own_gate[...] = cur_gate[...]

        @pl.when(s == 0)
        def _():
            own[...] = own[...] + cur[...]
            own_gate[...] = own_gate[...] + cur_gate[...]

        return 0

    lax.fori_loop(0, STEPS, second_pass, 0)

    def query_pass(c, _):
        cols = pl.ds(pl.multiple_of(c * 256, 256), 256)
        acc = jnp.dot(wt_all[...], ds_all[:, cols], preferred_element_type=F32) * SCALE
        for q in range(2):
            for h in range(2):
                tile = acc[q * SPAN:(q + 1) * SPAN, h * SPAN:(h + 1) * SPAN].T
                lanes = pl.ds(pl.multiple_of(c * 256 + h * SPAN, SPAN), SPAN)
                dq_ref[q * SPAN:(q + 1) * SPAN, lanes] = tile.astype(BF16)
        return 0

    lax.fori_loop(0, 4, query_pass, 0)

    def collect(ref):
        key_part, value_part, gate_part = unpack(ref)
        own[0:256, :] = own[0:256, :] + key_part
        own[256:512, :] = own[256:512, :] + value_part
        own_gate[...] = own_gate[...] + gate_part

    pre_copy(0).wait_recv()
    collect(pre_in.at[0])

    def receive(i, _):
        j = CHIPS - 1 - i
        sum_copy(j).wait_recv()
        collect(sum_in.at[j])
        return 0

    lax.fori_loop(0, CHIPS - 1, receive, 0)
    dk_ref[...] = own[0:256, :].astype(BF16)
    dv_ref[...] = own[256:512, :].astype(BF16)
    gates = gate_ref[0:8, :].astype(F32)
    dg_ref[...] = -own_gate[...] / (1.0 + jnp.exp(-gates))

    for j in range(CHIPS):
        own_copy(j).wait_send()
        pre_copy(j).wait_send()
    for j in range(1, CHIPS):
        forward_copy(j).wait_send()
        sum_copy(jnp.int32(j)).wait_send()


def on_device(queries, keys, values, gate_logit, out_grad, stretch_place):
    rows = 2 * SPAN
    gates = jnp.pad(gate_logit.reshape(2, SPAN), ((0, 14), (0, 0)))
    vmem = pl.BlockSpec(memory_space=pltpu.VMEM)
    dma = pltpu.SemaphoreType.DMA
    dq, dk, dv, dg = pl.pallas_call(
        kernel,
        out_shape=(
            jax.ShapeDtypeStruct((rows, WIDE), BF16),
            jax.ShapeDtypeStruct((rows, SPAN), BF16),
            jax.ShapeDtypeStruct((rows, SPAN), BF16),
            jax.ShapeDtypeStruct((8, SPAN), F32),
        ),
        in_specs=[pl.BlockSpec(memory_space=pltpu.SMEM)] + [vmem] * 5,
        out_specs=(vmem,) * 4,
        scratch_shapes=[
            pltpu.VMEM((2 * CHIPS, ROWS, SPAN), BF16),
            pltpu.VMEM((WIDE, rows), BF16),
            pltpu.VMEM((rows, WIDE), BF16),
            pltpu.VMEM((WIDE, rows), BF16),
            pltpu.VMEM((rows, WIDE), BF16),
            pltpu.VMEM((rows, STEPS * rows), BF16),
            pltpu.VMEM((STEPS, rows, WIDE), F32),
            pltpu.VMEM((STEPS, rows, WIDE), F32),
            pltpu.VMEM((STEPS, 8, WIDE), F32),
            pltpu.VMEM((8, WIDE), F32),
            pltpu.VMEM((STEPS * rows, WIDE), BF16),
            pltpu.VMEM((2 * rows, SPAN), F32),
            pltpu.VMEM((8, SPAN), F32),
            pltpu.VMEM((2 * rows, SPAN), F32),
            pltpu.VMEM((8, SPAN), F32),
            pltpu.VMEM((CHIPS, ROWS, SPAN), BF16),
            pltpu.VMEM((CHIPS, ROWS, SPAN), BF16),
            pltpu.VMEM((CHIPS, ROWS, SPAN), BF16),
            pltpu.VMEM((CHIPS, ROWS, SPAN), BF16),
            dma((CHIPS,)), dma((CHIPS,)), dma((2 * CHIPS,)),
            dma((CHIPS,)), dma((CHIPS,)), dma((CHIPS,)), dma((CHIPS,)),
        ],
        compiler_params=pltpu.CompilerParams(
            collective_id=0, has_side_effects=True, vmem_limit_bytes=62 * 1024 * 1024),
    )(stretch_place, queries, keys, values, gates, out_grad)
    return dq, dk, dv, dg[:2].reshape(rows, 1)


def solution(mesh):
    whole = P("ctx", "head")
    return jax.shard_map(
        on_device, mesh=mesh, in_specs=(whole,) * 5 + (P(),), out_specs=(whole,) * 4, check_vma=False)
```

time: 582 us -> 52.1 us (0.09)
  the two profiles are of different devices: /device:TPU:0 before, /device:TPU:68 now
where the time goes in v1:
time: 52.1 us; the launch traced here: 51.9 us
  Pallas kernels  45.3 us (87%)
  local copies, waits for them, and re-layouts  5.24 us (10%)
  other arithmetic  0.7 us (1%)
  between operations  0.64 us (1%)
    pallas_call x1, Pallas kernels, on_device(): pl.pallas_call(kernel, out_shape=(jax.ShapeDtypeStruct((rows, WIDE), BF16...  45.3 us
    unnamed x7, local copies, waits for them, and re-layouts  3.39 us
    slice x1, local copies, waits for them, and re-layouts, on_device(): return (dq, dk, dv, dg[:2].reshape(rows, 1))  1.25 us

profile of v1, /device:TPU:68, one launch (start us, length us, event | category | flops | bytes accessed | tf_op | source)
XLA Modules:
  0.0 51.9 jit_solution(4521570631234531886)
XLA Ops:
  0.6 0.7 %reduce = bf16[256]{0:T(256)(128)(2,1)S(1)} reduce(bf16[256,1]{0,1:T(2,128)(2,1)} %param.9, bf16[]{:T(256)} %constant.6), dimensions={1}, to_apply=%param.9.reduce_sub_computation | reduce | bytes 1026 | tf_op args[3]
  1.3 0.6 %pad.4.gate_ref = bf16[16,128]{1,0:T(8,128)(2,1)} pad(bf16[2,128]{1,0:T(2,128)(2,1)S(1)} %bitcast.2, bf16[]{:T(256)} %constant.2.clone.1), padding=0_14x0_0 | pad | bytes 4610 | tf_op jit(solution)/shard_map/jit(_pad)/pad | solution.py:335
  1.9 45.3 %shard_map.93 = (bf16[256,1024]{1,0:T(8,128)(2,1)}, bf16[256,128]{1,0:T(8,128)(2,1)}, bf16[256,128]{1,0:T(8,128)(2,1)}, f32[8,128]{1,0:T(8,128)}) custom-call(s32[32]{0:T(128)} %place.1, bf16[256,1024]{1,0:T(8,128)(2,1)} %q_ref.1, bf16[256,128]{1,0:T(8,128)(2,1)} %k_ref.1, bf16[256,128]{1,0:T(8,128)(2,1)} %v_ref.1, bf16[16,128]{1,0:T(8,128)(2,1)} %pad.4.gate_ref, ...), custom_call_target="tpu_custom_call" | custom-call | tf_op jit(solution)/shard_map/pallas_call | solution.py:338
  47.2 1.2 %slice.3 = f32[2,128]{1,0:T(2,128)} slice(f32[8,128]{1,0:T(8,128)} %get-tuple-element.11), slice={[0:2], [0:128]} | slice | bytes 2048 | tf_op jit(solution)/shard_map/slice | solution.py:374
  48.5 0.0 copy-start.1
  48.5 1.9 %copy.13 = bf16[256,1024]{1,0:T(8,128)(2,1)} copy(bf16[256,1024]{1,0:T(8,128)(2,1)} %get-tuple-element.16) | data formatting | bytes 1048576
  50.4 0.0 copy-done.1
  50.4 0.0 copy-start
  50.4 0.6 %copy.14 = bf16[256,128]{1,0:T(8,128)(2,1)} copy(bf16[256,128]{1,0:T(8,128)(2,1)S(1)} %copy-done.1) | data formatting | bytes 131072
  51.0 0.2 copy-done
  51.3 0.6 %copy.15 = bf16[256,128]{1,0:T(8,128)(2,1)} copy(bf16[256,128]{1,0:T(8,128)(2,1)S(1)} %copy-done) | data formatting | bytes 131072
Async XLA Ops:
  48.5 1.9 %copy-start.1 = (bf16[256,128]{1,0:T(8,128)(2,1)S(1)}, bf16[256,128]{1,0:T(8,128)(2,1)}, u32[]{:S(2)}) copy-start(bf16[256,128]{1,0:T(8,128)(2,1)} %get-tuple-element.17) | copy-start | bytes 196612
  50.4 0.9 %copy-start = (bf16[256,128]{1,0:T(8,128)(2,1)S(1)}, bf16[256,128]{1,0:T(8,128)(2,1)}, u32[]{:S(2)}) copy-start(bf16[256,128]{1,0:T(8,128)(2,1)} %get-tuple-element.18) | copy-start | bytes 196612

commit v2 on v1

--- a/solution.py
+++ b/solution.py
@@ -21,80 +21,110 @@
 F32, BF16 = jnp.float32, jnp.bfloat16
 
 
-def step_slot(s):
-    half, odd = lax.div(s, 2), lax.rem(s, 2)
-    first = lax.div(1, half + 1)
-    return 2 * half - odd - lax.div(s, 16) + first * odd
-
-
-def forward_step(i):
-    half, odd = lax.div(i, 2), lax.rem(i, 2)
-    second = lax.div(2, half + 1) - 2 * lax.div(1, half + 1)
-    return i + second * (1 - 2 * odd)
+FIRST = (0, 1, 2, 3, 7, 9, 4, 8, 10, 5, 6, 11, 15, 12, 16, 13, 14)
+SECOND = (14, 12, 13, 16, 11, 6, 15, 10, 5, 4, 9, 8, 3, 2, 7, 1, 0)
+KEY, VALUE = pl.ds(0, 256), pl.ds(256, 272)
+PARTS = (KEY, VALUE)
+
+
+def table(values, i):
+    out = i * 0 + values[0]
+    for at, value in enumerate(values[1:], 1):
+        out = jnp.where(i == at, value, out)
+    return out
 
 
 def chip_at(y, x, j, sign):
-    dy, dx = lax.div(j, 4), lax.rem(j, 4)
+    dy, dx = (j // 4, j % 4) if isinstance(j, int) else (lax.div(j, 4), lax.rem(j, 4))
     return lax.rem(y + 2 + sign * dy, 2) * 4 + lax.rem(x + 4 + sign * dx, 4)
 
 
 def kernel(
     place, q_ref, k_ref, v_ref, gate_ref, o_ref,
     dq_ref, dk_ref, dv_ref, dg_ref,
-    blocks, qc, qct, oc, oct_, wt_all, e_all, p_all, stat, total, ds_all,
-    cur, cur_gate, own, own_gate, pre_out, pre_in, sum_out, sum_in,
-    own_send, fwd_send, block_recv, pre_send, pre_recv, sum_send, sum_recv,
+    blocks, q_in, o_in, qc, qct, oc, oct_, wt_all, e_all, p_all, stat, total, ds_all,
+    cur, cur_gate, own, own_gate, held, held_gate, pre_out, pre_in, sum_out, sum_in,
+    dq_out, dk_out, dv_out, dg_out,
+    in_sem, out_sem, block_send, block_recv, pre_send, pre_recv, sum_send, sum_recv,
 ):
     me = lax.axis_index("ctx")
     core = lax.rem(me, 2)
     chip = lax.div(me, 2)
     y, x = lax.div(chip, 4), lax.rem(chip, 4)
     partner = me + 1 - 2 * core
+    right = chip_at(y, x, 1, 1) * 2 + core
+    left = chip_at(y, x, 1, -1) * 2 + core
+    across = chip_at(y, x, 4, 1) * 2 + core
 
     barrier = pltpu.get_barrier_semaphore()
-    pl.semaphore_signal(barrier, inc=1, device_id={"ctx": partner}, device_id_type=MESH)
-    for j in range(1, CHIPS):
-        other = chip_at(y, x, jnp.int32(j), 1) * 2 + core
+    for other in (partner, right, left, across):
         pl.semaphore_signal(barrier, inc=1, device_id={"ctx": other}, device_id_type=MESH)
 
-    blocks[0, 0:256, :] = k_ref[...]
-    blocks[0, 256:512, :] = v_ref[...]
-    blocks[0, 512:528, :] = gate_ref[...]
-    pl.semaphore_wait(barrier, CHIPS)
-
-    def own_copy(j):
-        if j == 0:
-            target, slot = partner, 1
-        else:
-            target, slot = chip_at(y, x, jnp.int32(j), 1) * 2 + core, 2 * j
+    loads = [
+        pltpu.make_async_copy(k_ref, blocks.at[0, pl.ds(0, 256)], in_sem.at[0]),
+        pltpu.make_async_copy(v_ref, blocks.at[0, pl.ds(256, 256)], in_sem.at[1]),
+        pltpu.make_async_copy(q_ref, q_in, in_sem.at[2]),
+        pltpu.make_async_copy(o_ref, o_in, in_sem.at[3]),
+    ]
+    for load in loads:
+        load.start()
+    gate_row = gate_ref[...].astype(F32)
+    blocks[0, 512:528, :] = jnp.concatenate(
+        [gate_row[:, 0:128], gate_row[:, 128:256], jnp.zeros((14, SPAN), F32)], axis=0).astype(BF16)
+    pl.semaphore_wait(barrier, 4)
+
+    started = []
+
+    def block_copy(source, slot, part, target, sem):
         return pltpu.make_async_remote_copy(
-            src_ref=blocks.at[0], dst_ref=blocks.at[slot], send_sem=own_send.at[j],
-            recv_sem=block_recv.at[slot], device_id={"ctx": target}, device_id_type=MESH)
-
-    def forward_copy(j):
-        return pltpu.make_async_remote_copy(
-            src_ref=blocks.at[2 * j], dst_ref=blocks.at[2 * j + 1], send_sem=fwd_send.at[j],
-            recv_sem=block_recv.at[2 * j + 1], device_id={"ctx": partner}, device_id_type=MESH)
+            src_ref=blocks.at[source, PARTS[part]], dst_ref=blocks.at[slot, PARTS[part]], send_sem=block_send.at[sem],
+            recv_sem=block_recv.at[slot, part], device_id={"ctx": target}, device_id_type=MESH)
+
+    def send(*what):
+        started.append(what)
+        block_copy(*what).start()
+
+    def arrive(slot, part):
+        pltpu.make_async_remote_copy(
+            src_ref=blocks.at[slot, PARTS[part]], dst_ref=blocks.at[slot, PARTS[part]], send_sem=block_send.at[0],
+            recv_sem=block_recv.at[slot, part], device_id={"ctx": partner}, device_id_type=MESH).wait_recv()
+
+    def pass_on(slot, part):
+        arrive(slot, part)
+        send(slot, slot + 1, part, partner, 8 + slot + part)
+        if (slot, part) == (2, 0):
+            send(slot, 4, part, right, 24)
+        if (slot, part) == (6, 1):
+            send(slot, 4, part, left, 25)
+        if slot == 8:
+            send(slot, 10, part, right, 26 + part)
+            send(slot, 14, part, left, 28 + part)
+        if slot == 4:
+            send(slot, 12, part, across, 30 + part)
 
     def pre_copy(j):
         return pltpu.make_async_remote_copy(
             src_ref=pre_out.at[j], dst_ref=pre_in.at[j], send_sem=pre_send.at[j],
             recv_sem=pre_recv.at[j], device_id={"ctx": partner}, device_id_type=MESH)
 
-    def sum_copy(j):
-        target = chip_at(y, x, j, -1) * 2 + core
+    def sum_copy(j, part):
+        target = {1: left, 2: (left, right)[part], 3: right, 4: across, 5: left, 6: across, 7: right}[j]
         return pltpu.make_async_remote_copy(
-            src_ref=sum_out.at[j], dst_ref=sum_in.at[j], send_sem=sum_send.at[j],
-            recv_sem=sum_recv.at[j], device_id={"ctx": target}, device_id_type=MESH)
-
-    for j in range(CHIPS):
-        own_copy(j).start()
-
+            src_ref=sum_out.at[j, PARTS[part]], dst_ref=sum_in.at[j, PARTS[part]], send_sem=sum_send.at[j, part],
+            recv_sem=sum_recv.at[j, part], device_id={"ctx": target}, device_id_type=MESH)
+
+    for part in range(2):
+        loads[part].wait()
+        for at, (slot, target) in enumerate(((8, across), (2, right), (6, left), (1, partner))):
+            send(0, slot, part, target, 2 * at + part)
+
+    loads[2].wait()
+    loads[3].wait()
     for h in range(HEADS):
         wide = slice(h * SPAN, (h + 1) * SPAN)
         for q in range(2):
             part = slice(q * SPAN, (q + 1) * SPAN)
-            for src, plain, turned in ((q_ref, qc, qct), (o_ref, oc, oct_)):
+            for src, plain, turned in ((q_in, qc, qct), (o_in, oc, oct_)):
                 tile = src[part, wide]
                 plain[wide, part] = tile
                 turned[part, wide] = tile.T
@@ -107,7 +137,7 @@
     q_high = (a1 > a0).astype(jnp.int32)
 
     def pairs(s):
-        slot = step_slot(s)
+        slot = jnp.maximum(s - 1, 0)
         theirs = chip_at(y, x, lax.div(slot, 2), -1) * 2 + lax.rem(core + slot, 2)
         b0, b1 = place[2 * theirs], place[2 * theirs + 1]
         k_low = (b1 < b0).astype(jnp.int32)
@@ -131,18 +161,42 @@
         return lax.select(first, a, b)
 
     def first_pass(i, _):
-        s = forward_step(i)
+        s = table(FIRST, i)
         slot, units = pairs(s)
 
-        @pl.when(s >= 2)
-        def _():
-            pltpu.make_async_remote_copy(
-                src_ref=blocks.at[slot], dst_ref=blocks.at[slot], send_sem=own_send.at[0],
-                recv_sem=block_recv.at[slot], device_id={"ctx": partner}, device_id_type=MESH).wait_recv()
-
-            @pl.when(lax.rem(slot, 2) == 0)
-            def _():
-                forward_copy(lax.div(slot, 2)).start()
+        @pl.when(i == 2)
+        def _():
+            arrive(1, 0)
+            arrive(1, 1)
+
+        @pl.when(i == 3)
+        def _():
+            for slot, part in ((2, 0), (8, 0), (6, 0), (6, 1), (8, 1), (2, 1)):
+                pass_on(slot, part)
+
+        @pl.when(i == 6)
+        def _():
+            pass_on(4, 0)
+
+        @pl.when(i == 8)
+        def _():
+            pass_on(4, 1)
+
+        @pl.when(i == 11)
+        def _():
+            for part in range(2):
+                pass_on(10, part)
+                pass_on(14, part)
+
+        @pl.when(i == 14)
+        def _():
+            for part in range(2):
+                pass_on(12, part)
+
+        @pl.when(jnp.logical_and(i >= 6, lax.rem(slot, 2) == 1))
+        def _():
+            arrive(slot, 0)
+            arrive(slot, 1)
 
         k0, k1 = blocks[slot, 0:128, :].astype(F32), blocks[slot, 128:256, :].astype(F32)
         v0, v1 = blocks[slot, 256:384, :].astype(F32), blocks[slot, 384:512, :].astype(F32)
@@ -205,18 +259,45 @@
     total[2:4, :] = 1.0 / mass
     total[4:6, :] = weighted / mass
 
-    def pack(dst, key_part, value_part, gate_part):
-        dst[0:256, :] = key_part.astype(BF16)
-        dst[256:512, :] = value_part.astype(BF16)
-        high = gate_part.astype(BF16).astype(F32)
-        dst[512:528, :] = jnp.concatenate([high, gate_part - high], axis=0).astype(BF16)
-
-    def unpack(src):
+    def pack(dst, part, rows, gate_rows=None):
+        if part == 0:
+            dst[0:256, :] = rows.astype(BF16)
+        else:
+            dst[256:512, :] = rows.astype(BF16)
+            high = gate_rows.astype(BF16).astype(F32)
+            dst[512:528, :] = jnp.concatenate([high, gate_rows - high], axis=0).astype(BF16)
+
+    def unpack_keys(src):
+        return src[0:256, :].astype(F32)
+
+    def unpack_values(src):
         tail = src[512:528, :].astype(F32)
-        return src[0:256, :].astype(F32), src[256:512, :].astype(F32), tail[0:8] + tail[8:16]
+        return src[256:512, :].astype(F32), tail[0:8] + tail[8:16]
+
+    def leave(j, part, rows, gate_rows):
+        if part == 0:
+            pack(sum_out.at[j], 0, rows[0:256, :])
+        else:
+            pack(sum_out.at[j], 1, rows[256:512, :], gate_rows[...])
+        sum_copy(j, part).start()
+
+    def join(j, part, others):
+        rows, gate_rows = held.at[j - 1], held_gate.at[j - 1]
+        for other in others:
+            sum_copy(other, part).wait_recv()
+            add(rows, gate_rows, part, sum_in.at[other])
+        leave(j, part, rows, gate_rows)
+
+    def add(rows, gate_rows, part, src):
+        if part == 0:
+            rows[0:256, :] = rows[0:256, :] + unpack_keys(src)
+        else:
+            more, gate_more = unpack_values(src)
+            rows[256:512, :] = rows[256:512, :] + more
+            gate_rows[...] = gate_rows[...] + gate_more
 
     def second_pass(i, _):
-        s = STEPS - 1 - i
+        s = table(SECOND, i)
         slot, units = pairs(s)
         j = lax.div(slot, 2)
         scale_rows, delta_rows = [], []
@@ -265,15 +346,37 @@
 
         @pl.when(lax.rem(slot, 2) == 1)
         def _():
-            pack(pre_out.at[j], cur[0:256, :], cur[256:512, :], cur_gate[...])
+            pack(pre_out.at[j], 0, cur[0:256, :])
+            pack(pre_out.at[j], 1, cur[256:512, :], cur_gate[...])
             pre_copy(j).start()
 
         @pl.when(jnp.logical_and(lax.rem(slot, 2) == 0, s >= 2))
         def _():
             pre_copy(j).wait_recv()
-            more = unpack(pre_in.at[j])
-            pack(sum_out.at[j], cur[0:256, :] + more[0], cur[256:512, :] + more[1], cur_gate[...] + more[2])
-            sum_copy(j).start()
+            cur[0:256, :] = cur[0:256, :] + unpack_keys(pre_in.at[j])
+            more, gate_more = unpack_values(pre_in.at[j])
+            cur[256:512, :] = cur[256:512, :] + more
+            cur_gate[...] = cur_gate[...] + gate_more
+
+        for at in range(1, CHIPS):
+            @pl.when(s == 2 * at + 1)
+            def _():
+                for part in range(2):
+                    if at in (5, 6, 7) or (at, part) in ((1, 1), (3, 0)):
+                        leave(at, part, cur, cur_gate)
+                if at in (1, 2, 3, 4):
+                    held[at - 1] = cur[...]
+                    held_gate[at - 1] = cur_gate[...]
+
+        @pl.when(i == 10)
+        def _():
+            for part in range(2):
+                join(2, part, (6,))
+
+        @pl.when(i == 14)
+        def _():
+            for part in range(2):
+                join(4, part, (5, 7))
 
         @pl.when(s == 1)
         def _():
@@ -288,6 +391,8 @@
         return 0
 
     lax.fori_loop(0, STEPS, second_pass, 0)
+    join(1, 0, (2,))
+    join(3, 1, (2,))
 
     def query_pass(c, _):
         cols = pl.ds(pl.multiple_of(c * 256, 256), 256)
@@ -296,57 +401,78 @@
             for h in range(2):
                 tile = acc[q * SPAN:(q + 1) * SPAN, h * SPAN:(h + 1) * SPAN].T
                 lanes = pl.ds(pl.multiple_of(c * 256 + h * SPAN, SPAN), SPAN)
-                dq_ref[q * SPAN:(q + 1) * SPAN, lanes] = tile.astype(BF16)
+                dq_out[q * SPAN:(q + 1) * SPAN, lanes] = tile.astype(BF16)
         return 0
 
     lax.fori_loop(0, 4, query_pass, 0)
 
-    def collect(ref):
-        key_part, value_part, gate_part = unpack(ref)
-        own[0:256, :] = own[0:256, :] + key_part
-        own[256:512, :] = own[256:512, :] + value_part
-        own_gate[...] = own_gate[...] + gate_part
-
+    stores = [
+        pltpu.make_async_copy(dq_out, dq_ref, out_sem.at[0]),
+        pltpu.make_async_copy(dk_out, dk_ref, out_sem.at[1]),
+        pltpu.make_async_copy(dv_out, dv_ref, out_sem.at[2]),
+        pltpu.make_async_copy(dg_out, dg_ref, out_sem.at[3]),
+    ]
+    stores[0].start()
     pre_copy(0).wait_recv()
-    collect(pre_in.at[0])
-
-    def receive(i, _):
-        j = CHIPS - 1 - i
-        sum_copy(j).wait_recv()
-        collect(sum_in.at[j])
-        return 0
-
-    lax.fori_loop(0, CHIPS - 1, receive, 0)
-    dk_ref[...] = own[0:256, :].astype(BF16)
-    dv_ref[...] = own[256:512, :].astype(BF16)
-    gates = gate_ref[0:8, :].astype(F32)
-    dg_ref[...] = -own_gate[...] / (1.0 + jnp.exp(-gates))
-
+    for part in range(2):
+        add(own, own_gate, part, pre_in.at[0])
+    for part in range(2):
+        for j in (1, 3, 4):
+            sum_copy(j, part).wait_recv()
+            add(own, own_gate, part, sum_in.at[j])
+        if part == 0:
+            dk_out[...] = own[0:256, :].astype(BF16)
+            stores[1].start()
+    dv_out[...] = own[256:512, :].astype(BF16)
+    gate_sum = jnp.concatenate([own_gate[0:1, :], own_gate[1:2, :]], axis=1)
+    dg_out[...] = -gate_sum / (1.0 + jnp.exp(-gate_ref[...].astype(F32)))
+    stores[2].start()
+    stores[3].start()
+
+    for what in started:
+        block_copy(*what).wait_send()
     for j in range(CHIPS):
-        own_copy(j).wait_send()
         pre_copy(j).wait_send()
     for j in range(1, CHIPS):
-        forward_copy(j).wait_send()
-        sum_copy(jnp.int32(j)).wait_send()
+        for part in range(2):
+            sum_copy(j, part).wait_send()
+    for store in stores:
+        store.wait()
+
+
+def hand_over(*refs):
+    sources, targets, held, sem_in, sem_out = refs[0:4], refs[4:8], refs[8:12], refs[12], refs[13]
+    pulls = [pltpu.make_async_copy(sources[n], held[n], sem_in.at[n]) for n in range(4)]
+    pushes = [pltpu.make_async_copy(held[n], targets[n], sem_out.at[n]) for n in range(4)]
+    for pull in pulls:
+        pull.start()
+    for pull, push in zip(pulls, pushes):
+        pull.wait()
+        push.start()
+    for push in pushes:
+        push.wait()
 
 
 def on_device(queries, keys, values, gate_logit, out_grad, stretch_place):
     rows = 2 * SPAN
-    gates = jnp.pad(gate_logit.reshape(2, SPAN), ((0, 14), (0, 0)))
     vmem = pl.BlockSpec(memory_space=pltpu.VMEM)
+    anywhere = pl.BlockSpec(memory_space=pl.ANY)
     dma = pltpu.SemaphoreType.DMA
-    dq, dk, dv, dg = pl.pallas_call(
+    outs = (
+        jax.ShapeDtypeStruct((rows, WIDE), BF16),
+        jax.ShapeDtypeStruct((rows, SPAN), BF16),
+        jax.ShapeDtypeStruct((rows, SPAN), BF16),
+        jax.ShapeDtypeStruct((1, rows), F32),
+    )
+    results = pl.pallas_call(
         kernel,
-        out_shape=(
-            jax.ShapeDtypeStruct((rows, WIDE), BF16),
-            jax.ShapeDtypeStruct((rows, SPAN), BF16),
-            jax.ShapeDtypeStruct((rows, SPAN), BF16),
-            jax.ShapeDtypeStruct((8, SPAN), F32),
-        ),
-        in_specs=[pl.BlockSpec(memory_space=pltpu.SMEM)] + [vmem] * 5,
-        out_specs=(vmem,) * 4,
+        out_shape=outs,
+        in_specs=[pl.BlockSpec(memory_space=pltpu.SMEM), anywhere, anywhere, anywhere, vmem, anywhere],
+        out_specs=(anywhere,) * 4,
         scratch_shapes=[
             pltpu.VMEM((2 * CHIPS, ROWS, SPAN), BF16),
+            pltpu.VMEM((rows, WIDE), BF16),
+            pltpu.VMEM((rows, WIDE), BF16),
             pltpu.VMEM((WIDE, rows), BF16),
             pltpu.VMEM((rows, WIDE), BF16),
             pltpu.VMEM((WIDE, rows), BF16),
@@ -361,17 +487,31 @@
             pltpu.VMEM((8, SPAN), F32),
             pltpu.VMEM((2 * rows, SPAN), F32),
             pltpu.VMEM((8, SPAN), F32),
+            pltpu.VMEM((4, 2 * rows, SPAN), F32),
+            pltpu.VMEM((4, 8, SPAN), F32),
             pltpu.VMEM((CHIPS, ROWS, SPAN), BF16),
             pltpu.VMEM((CHIPS, ROWS, SPAN), BF16),
             pltpu.VMEM((CHIPS, ROWS, SPAN), BF16),
             pltpu.VMEM((CHIPS, ROWS, SPAN), BF16),
-            dma((CHIPS,)), dma((CHIPS,)), dma((2 * CHIPS,)),
-            dma((CHIPS,)), dma((CHIPS,)), dma((CHIPS,)), dma((CHIPS,)),
+            pltpu.VMEM((rows, WIDE), BF16),
+            pltpu.VMEM((rows, SPAN), BF16),
+            pltpu.VMEM((rows, SPAN), BF16),
+            pltpu.VMEM((1, rows), F32),
+            dma((4,)), dma((4,)), dma((32,)), dma((2 * CHIPS, 2)),
+            dma((CHIPS,)), dma((CHIPS,)), dma((CHIPS, 2)), dma((CHIPS, 2)),
         ],
         compiler_params=pltpu.CompilerParams(
             collective_id=0, has_side_effects=True, vmem_limit_bytes=62 * 1024 * 1024),
-    )(stretch_place, queries, keys, values, gates, out_grad)
-    return dq, dk, dv, dg[:2].reshape(rows, 1)
+    )(stretch_place, queries, keys, values, gate_logit.T, out_grad)
+    dq, dk, dv, dg = pl.pallas_call(
+        hand_over,
+        out_shape=outs,
+        in_specs=[anywhere] * 4,
+        out_specs=(anywhere,) * 4,
+        scratch_shapes=[pltpu.VMEM(out.shape, out.dtype) for out in outs] + [dma((4,)), dma((4,))],
+        compiler_params=pltpu.CompilerParams(vmem_limit_bytes=62 * 1024 * 1024),
+    )(*results)
+    return dq, dk, dv, dg.T
 
 
 def solution(mesh):

time: 52.1 us -> 39.4 us (0.76)
  the two profiles are of different devices: /device:TPU:68 before, /device:TPU:0 now
where the time goes in v2:
time: 39.4 us; the launch traced here: 39.1 us
  Pallas kernels  38.5 us (98%)
  between operations  0.64 us (2%)
    pallas_call x1, Pallas kernels, on_device(): pl.pallas_call(kernel, out_shape=outs, in_specs=[pl.BlockSpec(memory_spac...  36.5 us
    pallas_call x1, Pallas kernels, on_device(): pl.pallas_call(hand_over, out_shape=outs, in_specs=[anywhere] * 4, out_sp...  1.94 us

profile of v2, /device:TPU:0, one launch (start us, length us, event | category | flops | bytes accessed | tf_op | source)
XLA Modules:
  0.0 39.1 jit_solution(16842154878576228555)
XLA Ops:
  0.6 36.5 %shard_map.93 = (bf16[256,1024]{1,0:T(8,128)(2,1)}, bf16[256,128]{1,0:T(8,128)(2,1)}, bf16[256,128]{1,0:T(8,128)(2,1)}, f32[1,256]{1,0:T(1,128)}) custom-call(s32[32]{0:T(128)} %place.1, bf16[256,1024]{1,0:T(8,128)(2,1)} %q_ref.1, bf16[256,128]{1,0:T(8,128)(2,1)} %k_ref.1, bf16[256,128]{1,0:T(8,128)(2,1)} %v_ref.1, bf16[1,256]{1,0:T(2,128)(2,1)} %bitcast.2, ...), custom_call_target="tpu_custom_call" | custom-call | tf_op jit(solution)/shard_map/pallas_call | solution.py:467
  37.2 1.9 %shard_map.94 = (bf16[256,1024]{1,0:T(8,128)(2,1)}, bf16[256,128]{1,0:T(8,128)(2,1)}, bf16[256,128]{1,0:T(8,128)(2,1)}, f32[1,256]{1,0:T(1,128)}) custom-call(bf16[256,1024]{1,0:T(8,128)(2,1)} %get-tuple-element.12.refs_0_, bf16[256,128]{1,0:T(8,128)(2,1)} %get-tuple-element.13.refs_1_, bf16[256,128]{1,0:T(8,128)(2,1)} %get-tuple-element.14.refs_2_, ...), custom_call_target="tpu_custom_call" | custom-call | tf_op jit(solution)/shard_map/pallas_call | solution.py:506

commit v3 on v1

v3 whole, which is shorter than its diff:
```python
import functools

import jax
import jax.numpy as jnp
from jax import lax
from jax.experimental import pallas as pl
from jax.experimental.pallas import tpu as pltpu
from jax.sharding import PartitionSpec as P

DELAY = 256
SPAN = 128
HEADS = 8
WIDE = SPAN * HEADS
CHIPS = 8
ROWS = 528
NEG = -1e30
LOG2E = 1.4426950408889634
SCALE = 128 ** (-0.5)
MESH = pl.DeviceIdType.MESH
F32, BF16 = jnp.float32, jnp.bfloat16


FIRST = ((0, 2, 8, 7, 4, 10, 11, 12), (1, 6, 3, 9, 5, 14, 15, 13))
SECOND = ((13, 12, 10, 14, 4, 8, 2, 6), (11, 15, 5, 9, 3, 7, 1, 0))
CROSS = 16
LATER = tuple(2 * (SECOND[0] if s in SECOND[0] else SECOND[1]).index(s) + (s in SECOND[1]) for s in range(CROSS))
PAIRS = 33
PARTS = (pl.ds(0, 256), pl.ds(256, 272))
QUARTERS = (pl.ds(0, 128), pl.ds(128, 128), pl.ds(256, 128), pl.ds(384, 144))


def table(values, i):
    out = i * 0 + values[0]
    for at, value in enumerate(values[1:], 1):
        out = jnp.where(i == at, value, out)
    return out


def chip_at(y, x, j, sign):
    dy, dx = (j // 4, j % 4) if isinstance(j, int) else (lax.div(j, 4), lax.rem(j, 4))
    return lax.rem(y + 2 + sign * dy, 2) * 4 + lax.rem(x + 4 + sign * dx, 4)


def kernel(
    place, q_ref, k_ref, v_ref, gate_ref, o_ref,
    dq_ref, dk_ref, dv_ref, dg_ref,
    blocks, qc, oc, wt_all, e_all, p_all, stat, total,
    cur, cur_gate, own, own_gate, held, held_gate, pre_out, pre_in, sum_out, sum_in,
    in_sem, block_send, block_recv, pre_send, pre_recv, sum_send, sum_recv,
):
    me = lax.axis_index("ctx")
    core = lax.rem(me, 2)
    chip = lax.div(me, 2)
    y, x = lax.div(chip, 4), lax.rem(chip, 4)
    partner = me + 1 - 2 * core
    right = chip_at(y, x, 1, 1) * 2 + core
    left = chip_at(y, x, 1, -1) * 2 + core
    across = chip_at(y, x, 4, 1) * 2 + core

    barrier = pltpu.get_barrier_semaphore()
    for other in (partner, right, left, across):
        pl.semaphore_signal(barrier, inc=1, device_id={"ctx": other}, device_id_type=MESH)

    def recv_sem(slot, part):
        return block_recv.at[16 + slot // 2 if part == 1 and slot in (2, 4, 6, 8) else slot]

    def send(source, slot, part, target):
        pltpu.make_async_remote_copy(
            src_ref=blocks.at[source, PARTS[part]], dst_ref=blocks.at[slot, PARTS[part]], send_sem=block_send,
            recv_sem=recv_sem(slot, part), device_id={"ctx": target}, device_id_type=MESH).start()

    def arrive(slot, part=None):
        where = blocks.at[slot] if part is None else blocks.at[slot, PARTS[part]]
        pltpu.make_async_remote_copy(
            src_ref=where, dst_ref=where, send_sem=block_send, recv_sem=recv_sem(slot, part or 0),
            device_id={"ctx": partner}, device_id_type=MESH).wait_recv()

    def pass_on(slot):
        for part in range(2):
            send(slot, slot + 1, part, partner)

    def pre_copy(j):
        return pltpu.make_async_remote_copy(
            src_ref=pre_out.at[j], dst_ref=pre_in.at[j], send_sem=pre_send,
            recv_sem=pre_recv.at[j], device_id={"ctx": partner}, device_id_type=MESH)

    def sum_copy(j, part):
        target = {1: left, 2: left if part < 2 else right, 3: right, 4: across, 5: left, 6: across, 7: right}[j]
        return pltpu.make_async_remote_copy(
            src_ref=sum_out.at[j - 1, QUARTERS[part]], dst_ref=sum_in.at[j - 1, QUARTERS[part]], send_sem=sum_send,
            recv_sem=sum_recv.at[j - 1, part], device_id={"ctx": target}, device_id_type=MESH)

    key_row = lax.broadcasted_iota(jnp.int32, (SPAN, SPAN), 0)
    query_col = lax.broadcasted_iota(jnp.int32, (SPAN, SPAN), 1)
    lag = query_col - key_row
    a0, a1 = place[2 * me], place[2 * me + 1]
    a_low = jnp.minimum(a0, a1)
    q_high = (a1 > a0).astype(jnp.int32)

    def block_of(slot):
        theirs = chip_at(y, x, lax.div(slot, 2), -1) * 2 + lax.rem(core + slot, 2)
        b0, b1 = place[2 * theirs], place[2 * theirs + 1]
        return b0, b1, (b1 < b0).astype(jnp.int32)

    def described(k, q, b0, b1):
        apart = jnp.where(q == 0, a0, a1) - jnp.where(k == 0, b0, b1)
        return k, q, DELAY - SPAN * apart, -SPAN * apart

    def pairs(s):
        b0, b1, k_low = block_of(s)
        below = jnp.minimum(b0, b1) < a_low
        diag = s == 0
        k0 = jnp.where(diag, 0, jnp.where(below, k_low, 0))
        k1 = jnp.where(diag, 1, jnp.where(below, k_low, 1))
        q0 = jnp.where(diag, 0, jnp.where(below, 0, q_high))
        q1 = jnp.where(diag, 1, jnp.where(below, 1, q_high))
        return described(k0, q0, b0, b1), described(k1, q1, b0, b1)

    def pair_across():
        b0, b1, k_low = block_of(core * 0)
        return (described(k_low, q_high, b0, b1),)

    def take(first, a, b):
        return lax.select(first, a, b)

    def scores_of(work, group):
        qct, oct_, raw_s, raw_g = work
        zero = jnp.zeros((SPAN, SPAN), F32)
        wk, wv, todo = [], [], []
        for s, slot, units in group:
            where = s if s is CROSS else table(LATER, s)
            k0, k1 = blocks[slot, 0:128, :].astype(F32), blocks[slot, 128:256, :].astype(F32)
            v0, v1 = blocks[slot, 256:384, :].astype(F32), blocks[slot, 384:512, :].astype(F32)
            gates = blocks[slot, 512:528, :].astype(F32)
            evict = -LOG2E * (jnp.maximum(gates, 0.0) + jnp.log(1.0 + jnp.exp(-jnp.abs(gates))))
            for u, (k, q, least, live) in enumerate(units):
                ku, vu = take(k == 0, k0, k1), take(k == 0, v0, v1)
                wk.append(jnp.concatenate([take(q == 0, ku, zero), take(q == 0, zero, ku)], axis=1).astype(BF16))
                wv.append(jnp.concatenate([take(q == 0, vu, zero), take(q == 0, zero, vu)], axis=1).astype(BF16))
                kt = ku.T
                columns = pl.ds(pl.multiple_of(where * 256 + u * SPAN, SPAN), SPAN)
                wt_all[0:128, columns] = take(q == 0, kt, zero).astype(BF16)
                wt_all[128:256, columns] = take(q == 0, zero, kt).astype(BF16)
                column = jnp.broadcast_to(take(k == 0, evict[0:1, :], evict[1:2, :]), (SPAN, SPAN)).T
                bias = jnp.where(lag >= least, column, 0.0)
                if s is not CROSS:
                    bias = jnp.where(lag >= live, bias, NEG)
                todo.append((s, u, bias))
        wk, wv = jnp.concatenate(wk, axis=0), jnp.concatenate(wv, axis=0)
        height = len(todo) * SPAN
        for c in range(4):
            cols = slice(c * 256, (c + 1) * 256)
            raw_s[c, 0:height, :] = jnp.dot(wk, qct[:, cols], preferred_element_type=F32)
            raw_g[c, 0:height, :] = jnp.dot(wv, oct_[:, cols], preferred_element_type=F32)
            for at, (s, u, bias) in enumerate(todo):
                rows = slice(at * SPAN, (at + 1) * SPAN)
                for h in range(2):
                    lane = slice(h * SPAN, (h + 1) * SPAN)
                    wide = slice(c * 256 + h * SPAN, c * 256 + (h + 1) * SPAN)
                    score = (raw_s[c, rows, lane] * (SCALE * LOG2E) + bias).reshape(16, 8, SPAN)
                    grad = raw_g[c, rows, lane]
                    top = jnp.max(score, axis=0)
                    e = jnp.exp2(score - top[None])
                    e_all[2 * s + u, :, wide] = e.reshape(SPAN, SPAN)
                    p_all[2 * s + u, :, wide] = grad
                    stat[2 * s + u, 0, :, wide] = top
                    stat[2 * s + u, 1, :, wide] = jnp.sum(e, axis=0)
                    stat[2 * s + u, 2, :, wide] = jnp.sum(e * grad.reshape(16, 8, SPAN), axis=0)

    def first_pass(work, i, _):
        one, two = table(FIRST[0], i), table(FIRST[1], i)

        @pl.when(i == 0)
        def _():
            arrive(1)

        @pl.when(i == 1)
        def _():
            arrive(2, 0)
            send(2, 4, 0, right)
            arrive(6, 1)
            send(6, 4, 1, left)
            for part in range(2):
                arrive(8, part)
                send(8, 10, part, right)
                send(8, 14, part, left)
            arrive(2, 1)
            pass_on(2)
            arrive(6, 0)
            pass_on(6)
            pass_on(8)

        @pl.when(i == 2)
        def _():
            arrive(3)

        @pl.when(i == 3)
        def _():
            for part in range(2):
                arrive(4, part)
                send(4, 12, part, across)
            pass_on(4)
            arrive(7)
            arrive(9)

        @pl.when(i == 4)
        def _():
            arrive(5)

        @pl.when(i == 5)
        def _():
            for slot in (10, 14):
                arrive(slot)
                pass_on(slot)

        @pl.when(i == 6)
        def _():
            arrive(12)
            pass_on(12)
            arrive(11)
            arrive(15)

        @pl.when(i == 7)
        def _():
            arrive(13)

        scores_of(work, [(one, one, pairs(one)), (two, two, pairs(two))])
        return 0

    def first(q_in, o_in, qct, oct_, raw_s, raw_g):
        loads = [
            pltpu.make_async_copy(k_ref, blocks.at[0, pl.ds(0, 256)], in_sem.at[0]),
            pltpu.make_async_copy(v_ref, blocks.at[0, pl.ds(256, 256)], in_sem.at[1]),
            pltpu.make_async_copy(q_ref, q_in, in_sem.at[2]),
            pltpu.make_async_copy(o_ref, o_in, in_sem.at[3]),
        ]
        for load in loads:
            load.start()
        gate_row = gate_ref[...].astype(F32)
        blocks[0, 512:528, :] = jnp.concatenate(
            [gate_row[:, 0:128], gate_row[:, 128:256], jnp.zeros((14, SPAN), F32)], axis=0).astype(BF16)
        pl.semaphore_wait(barrier, 4)

        loads[0].wait()
        send(0, 2, 0, right)
        send(0, 8, 0, across)
        loads[1].wait()
        send(0, 6, 1, left)
        send(0, 2, 1, right)
        send(0, 8, 1, across)
        send(0, 6, 0, left)
        for part in range(2):
            send(0, 1, part, partner)

        loads[2].wait()
        loads[3].wait()
        for h in range(HEADS):
            wide = slice(h * SPAN, (h + 1) * SPAN)
            for q in range(2):
                part = slice(q * SPAN, (q + 1) * SPAN)
                for src, plain, turned in ((q_in, qc, qct), (o_in, oc, oct_)):
                    tile = src[part, wide]
                    plain[wide, part] = tile
                    turned[part, wide] = tile.T

        work = (qct, oct_, raw_s, raw_g)
        scores_of(work, [(CROSS, 0, pair_across())])
        lax.fori_loop(0, 8, functools.partial(first_pass, work), 0)

    turned, raw = pltpu.VMEM((2 * SPAN, WIDE), BF16), pltpu.VMEM((4, 512, 256), F32)
    pl.run_scoped(first, turned, turned, turned, turned, raw, raw)

    queries_of = [q for s in range(CROSS) for _, q, _, _ in pairs(s)] + [q_high]

    def combine(c, _):
        cols = pl.ds(pl.multiple_of(c * 256, 256), 256)
        tops = [jnp.full((8, 256), NEG, F32)] * 2
        for n, q in enumerate(queries_of):
            mine = stat[n, 0, :, cols]
            tops = [take(q == half, jnp.maximum(top, mine), top) for half, top in enumerate(tops)]
        tops = [jnp.broadcast_to(jnp.max(top, axis=0, keepdims=True), (8, 256)) for top in tops]
        mass = [jnp.zeros((8, 256), F32)] * 2
        weighted = [jnp.zeros((8, 256), F32)] * 2
        for n, q in enumerate(queries_of):
            factor = jnp.exp2(stat[n, 0, :, cols] - take(q == 0, tops[0], tops[1]))
            stat[n, 0, :, cols] = factor
            more = factor * stat[n, 1, :, cols]
            mass = [take(q == half, was + more, was) for half, was in enumerate(mass)]
            more = factor * stat[n, 2, :, cols]
            weighted = [take(q == half, was + more, was) for half, was in enumerate(weighted)]
        for half in range(2):
            inverse = 1.0 / jnp.broadcast_to(jnp.sum(mass[half], axis=0, keepdims=True), (8, 256))
            total[half, :, cols] = inverse
            total[2 + half, :, cols] = inverse * jnp.broadcast_to(jnp.sum(weighted[half], axis=0, keepdims=True), (8, 256))
        return 0

    lax.fori_loop(0, 4, combine, 0)

    def rows_of(part):
        return slice(part * SPAN, (part + 1) * SPAN)

    def pack(dst, part, rows, gate_rows):
        dst[rows_of(part), :] = rows[rows_of(part), :].astype(BF16)
        if part == 3:
            high = gate_rows[...].astype(BF16).astype(F32)
            dst[512:528, :] = jnp.concatenate([high, gate_rows[...] - high], axis=0).astype(BF16)

    def add(rows, gate_rows, part, src):
        rows[rows_of(part), :] = rows[rows_of(part), :] + src[rows_of(part), :].astype(F32)
        if part == 3:
            tail = src[512:528, :].astype(F32)
            gate_rows[...] = gate_rows[...] + tail[0:8] + tail[8:16]

    def leave(j, part, rows, gate_rows):
        pack(sum_out.at[j - 1], part, rows, gate_rows)
        sum_copy(j, part).start()

    def join(j, parts, others):
        rows, gate_rows = held.at[j - 1], held_gate.at[j - 1]
        for part in parts:
            for other in others:
                sum_copy(other, part).wait_recv()
                add(rows, gate_rows, part, sum_in.at[other - 1])
            leave(j, part, rows, gate_rows)

    def gradients_of(prob_low, grad_low, ds_all, place_at, group):
        todo = []
        for s, units in group:
            for u, (k, q, least, _) in enumerate(units):
                todo.append((2 * s + u, q == 0))
        height = len(todo) * SPAN
        gate_acc = [jnp.zeros((SPAN, SPAN), F32) for _ in todo]
        for c in range(4):
            cols = slice(c * 256, (c + 1) * 256)
            for at, (n, first) in enumerate(todo):
                factor = stat[n, 0, :, cols] * take(first, total[0, :, cols], total[1, :, cols])
                delta = take(first, total[2, :, cols], total[3, :, cols])
                prob = e_all[n, :, cols] * jnp.concatenate([factor] * 16, axis=0)
                grad = prob * (p_all[n, :, cols] - jnp.concatenate([delta] * 16, axis=0))
                gate_acc[at] = gate_acc[at] + grad[:, 0:128] + grad[:, 128:256]
                prob_low[at * SPAN:(at + 1) * SPAN, cols] = prob.astype(BF16)
                low = grad.astype(BF16)
                grad_low[at * SPAN:(at + 1) * SPAN, cols] = low
                ds_all[pl.ds(pl.multiple_of(place_at + at * SPAN, SPAN), SPAN), cols] = low
        value_acc = jnp.dot(prob_low[0:height, :], oc[...], preferred_element_type=F32)
        key_acc = jnp.dot(grad_low[0:height, :], qc[...], preferred_element_type=F32)
        zero = jnp.zeros((SPAN, SPAN), F32)
        at = 0
        for n, (s, units) in enumerate(group):
            key_out, value_out = [zero, zero], [zero, zero]
            gate_out = [jnp.zeros((1, SPAN), F32), jnp.zeros((1, SPAN), F32)]
            for k, q, least, _ in units:
                part = slice(at * SPAN, (at + 1) * SPAN)
                key_u = take(q == 0, key_acc[part, 0:128], key_acc[part, 128:256]) * SCALE
                value_u = take(q == 0, value_acc[part, 0:128], value_acc[part, 128:256])
                gate_u = jnp.sum(jnp.where(lag >= least, gate_acc[at], 0.0).T, axis=0, keepdims=True)
                for half in range(2):
                    hit = k == half
                    key_out[half] = key_out[half] + take(hit, key_u, zero)
                    value_out[half] = value_out[half] + take(hit, value_u, zero)
                    gate_out[half] = gate_out[half] + take(hit, gate_u, jnp.zeros((1, SPAN), F32))
                at += 1
            cur[n, 0:128, :] = key_out[0]
            cur[n, 128:256, :] = key_out[1]
            cur[n, 256:384, :] = value_out[0]
            cur[n, 384:512, :] = value_out[1]
            cur_gate[n] = jnp.concatenate(gate_out + [jnp.zeros((6, SPAN), F32)], axis=0)

    def to_partner(j, n):
        for part in range(4):
            pack(pre_out.at[j], part, cur.at[n], cur_gate.at[n])
        pre_copy(j).start()

    def from_partner(j, n):
        pre_copy(j).wait_recv()
        for part in range(4):
            add(cur.at[n], cur_gate.at[n], part, pre_in.at[j])

    def second_pass(prob_low, grad_low, ds_all, i, _):
        one, two = table(SECOND[0], i), table(SECOND[1], i)
        gradients_of(prob_low, grad_low, ds_all, i * 512, [(one, pairs(one)), (two, pairs(two))])

        @pl.when(i <= 6)
        def _():
            to_partner(lax.div(two, 2), 1)

        @pl.when(i == 0)
        def _():
            to_partner(lax.div(one, 2), 0)

        @pl.when(i >= 1)
        def _():
            from_partner(lax.div(one, 2), 0)

        @pl.when(i == 6)
        def _():
            join(2, (2, 3), (6,))

        for at in range(1, CHIPS):
            @pl.when(one == 2 * at)
            def _():
                for part in range(4):
                    if at in (5, 6, 7) or (at, part // 2) in ((1, 1), (3, 0)):
                        leave(at, part, cur.at[0], cur_gate.at[0])
                if at in (1, 2, 3, 4):
                    held[at - 1] = cur[0]
                    held_gate[at - 1] = cur_gate[0]

        @pl.when(i == 5)
        def _():
            join(2, (0, 1), (6,))

        @pl.when(i == 7)
        def _():
            own[...] = cur[1]
            own_gate[...] = cur_gate[1]

        return 0

    def query_pass(ds_all, c, _):
        @pl.when(c == 1)
        def _():
            join(4, (2, 3), (5, 7))

        @pl.when(c == 2)
        def _():
            join(1, (0, 1), (2,))
            join(3, (2, 3), (2,))

        cols = pl.ds(pl.multiple_of(c * 256, 256), 256)
        acc = jnp.dot(wt_all[...], ds_all[:, cols], preferred_element_type=F32) * SCALE
        for q in range(2):
            for h in range(2):
                tile = acc[q * SPAN:(q + 1) * SPAN, h * SPAN:(h + 1) * SPAN].T
                lanes = pl.ds(pl.multiple_of(c * 256 + h * SPAN, SPAN), SPAN)
                dq_ref[q * SPAN:(q + 1) * SPAN, lanes] = tile.astype(BF16)
        return 0

    def second(prob_low, grad_low, ds_all):
        lax.fori_loop(0, 8, functools.partial(second_pass, prob_low, grad_low, ds_all), 0)
        gradients_of(prob_low, grad_low, ds_all, CROSS * 256, [(CROSS, pair_across())])
        own[...] = own[...] + cur[0]
        own_gate[...] = own_gate[...] + cur_gate[0]
        join(4, (0, 1), (5, 7))
        lax.fori_loop(0, 4, functools.partial(query_pass, ds_all), 0)

    pl.run_scoped(second, pltpu.VMEM((512, WIDE), BF16), pltpu.VMEM((512, WIDE), BF16), pltpu.VMEM((PAIRS * SPAN, WIDE), BF16))

    pre_copy(0).wait_recv()
    for part in range(4):
        add(own, own_gate, part, pre_in.at[0])
    for j in (4, 1, 3):
        for part in range(4):
            sum_copy(j, part).wait_recv()
            add(own, own_gate, part, sum_in.at[j - 1])
    dk_ref[...] = own[0:256, :].astype(BF16)
    dv_ref[...] = own[256:512, :].astype(BF16)
    gate_sum = jnp.concatenate([own_gate[0:1, :], own_gate[1:2, :]], axis=1)
    dg_ref[...] = -gate_sum / (1.0 + jnp.exp(-gate_ref[...].astype(F32)))

    for sent, sem in ((blocks.at[pl.ds(0, 15)], block_send), (pre_out, pre_send), (sum_out, sum_send)):
        pltpu.make_async_remote_copy(
            src_ref=sent, dst_ref=sent, send_sem=sem, recv_sem=block_recv.at[0],
            device_id={"ctx": partner}, device_id_type=MESH).wait_send()


def hand_over(*refs):
    copies = [pltpu.make_async_copy(refs[n], refs[4 + n], refs[8].at[n]) for n in range(4)]
    for copy in copies:
        copy.start()
    for copy in copies:
        copy.wait()


def on_device(queries, keys, values, gate_logit, out_grad, stretch_place):
    rows = 2 * SPAN
    vmem = pl.BlockSpec(memory_space=pltpu.VMEM)
    anywhere = pl.BlockSpec(memory_space=pl.ANY)
    dma = pltpu.SemaphoreType.DMA
    outs = (
        jax.ShapeDtypeStruct((rows, WIDE), BF16),
        jax.ShapeDtypeStruct((rows, SPAN), BF16),
        jax.ShapeDtypeStruct((rows, SPAN), BF16),
        jax.ShapeDtypeStruct((1, rows), F32),
    )
    results = pl.pallas_call(
        kernel,
        out_shape=tuple(pltpu.VMEM(out.shape, out.dtype) for out in outs),
        in_specs=[pl.BlockSpec(memory_space=pltpu.SMEM), anywhere, anywhere, anywhere, vmem, anywhere],
        out_specs=(vmem,) * 4,
        scratch_shapes=[
            pltpu.VMEM((2 * CHIPS, ROWS, SPAN), BF16),
            pltpu.VMEM((WIDE, rows), BF16),
            pltpu.VMEM((WIDE, rows), BF16),
            pltpu.VMEM((rows, PAIRS * SPAN), BF16),
            pltpu.VMEM((PAIRS, SPAN, WIDE), F32),
            pltpu.VMEM((PAIRS, SPAN, WIDE), F32),
            pltpu.VMEM((PAIRS, 3, 8, WIDE), F32),
            pltpu.VMEM((4, 8, WIDE), F32),
            pltpu.VMEM((2, 2 * rows, SPAN), F32),
            pltpu.VMEM((2, 8, SPAN), F32),
            pltpu.VMEM((2 * rows, SPAN), F32),
            pltpu.VMEM((8, SPAN), F32),
            pltpu.VMEM((4, 2 * rows, SPAN), F32),
            pltpu.VMEM((4, 8, SPAN), F32),
            pltpu.VMEM((CHIPS, ROWS, SPAN), BF16),
            pltpu.VMEM((CHIPS, ROWS, SPAN), BF16),
            pltpu.VMEM((CHIPS - 1, ROWS, SPAN), BF16),
            pltpu.VMEM((CHIPS - 1, ROWS, SPAN), BF16),
            dma((4,)), dma, dma((21,)), dma, dma((CHIPS,)), dma, dma((CHIPS - 1, 4)),
        ],
        compiler_params=pltpu.CompilerParams(
            collective_id=0, has_side_effects=True, vmem_limit_bytes=63 * 1024 * 1024),
    )(stretch_place, queries, keys, values, gate_logit.T, out_grad)
    dq, dk, dv, dg = pl.pallas_call(
        hand_over,
        out_shape=outs,
        in_specs=[vmem] * 4,
        out_specs=(anywhere,) * 4,
        scratch_shapes=[dma((4,))],
        compiler_params=pltpu.CompilerParams(vmem_limit_bytes=1024 * 1024),
    )(*results)
    return dq, dk, dv, dg.T


def solution(mesh):
    whole = P("ctx", "head")
    return jax.shard_map(
        on_device, mesh=mesh, in_specs=(whole,) * 5 + (P(),), out_specs=(whole,) * 4, check_vma=False)
```

time: 52.1 us -> 35.8 us (0.69)
  the two profiles are of different devices: /device:TPU:68 before, /device:TPU:0 now
where the time goes in v3:
time: 35.8 us; the launch traced here: 35.7 us
  Pallas kernels  35 us (98%)
  between operations  0.64 us (2%)
    pallas_call x1, Pallas kernels, on_device(): pl.pallas_call(kernel, out_shape=tuple((pltpu.VMEM(out.shape, out.dtype)...  34.2 us
    pallas_call x1, Pallas kernels, on_device(): pl.pallas_call(hand_over, out_shape=outs, in_specs=[vmem] * 4, out_specs=...  0.86 us

profile of v3, /device:TPU:0, one launch (start us, length us, event | category | flops | bytes accessed | tf_op | source)
XLA Modules:
  0.0 35.7 jit_solution(13863571702897424153)
XLA Ops:
  0.6 34.2 %shard_map.93 = (bf16[256,1024]{1,0:T(8,128)(2,1)S(1)}, bf16[256,128]{1,0:T(8,128)(2,1)S(1)}, bf16[256,128]{1,0:T(8,128)(2,1)S(1)}, f32[1,256]{1,0:T(1,128)S(1)}) custom-call(s32[32]{0:T(128)} %place.1, bf16[256,1024]{1,0:T(8,128)(2,1)} %q_ref.1, bf16[256,128]{1,0:T(8,128)(2,1)} %k_ref.1, bf16[256,128]{1,0:T(8,128)(2,1)} %v_ref.1, bf16[1,256]{1,0:T(2,128)(2,1)} %bitcast.2, ...), custom_call_target="tpu_custom_call" | custom-call | tf_op jit(solution)/shard_map/pallas_call | solution.py:486
  34.8 0.9 %shard_map.94 = (bf16[256,1024]{1,0:T(8,128)(2,1)}, bf16[256,128]{1,0:T(8,128)(2,1)}, bf16[256,128]{1,0:T(8,128)(2,1)}, f32[1,256]{1,0:T(1,128)}) custom-call(bf16[256,1024]{1,0:T(8,128)(2,1)S(1)} %get-tuple-element.12.refs_0_, bf16[256,128]{1,0:T(8,128)(2,1)S(1)} %get-tuple-element.13.refs_1_, bf16[256,128]{1,0:T(8,128)(2,1)S(1)} %get-tuple-element.14.refs_2_, ...), custom_call_target="tpu_custom_call" | custom-call | tf_op jit(solution)/shard_map/pallas_call | solution.py:515

commit v4 on v3

--- a/solution.py
+++ b/solution.py
@@ -20,10 +20,11 @@
 F32, BF16 = jnp.float32, jnp.bfloat16
 
 
-FIRST = ((0, 2, 8, 7, 4, 10, 11, 12), (1, 6, 3, 9, 5, 14, 15, 13))
-SECOND = ((13, 12, 10, 14, 4, 8, 2, 6), (11, 15, 5, 9, 3, 7, 1, 0))
+FIRST = ((0, 2, 8, 7, 4, 10, 11), (1, 6, 3, 9, 5, 14, 15))
+SECOND = ((13, 12, 5, 4, 8, 2, 6), (11, 10, 9, 3, 7, 1, 0))
 CROSS = 16
-LATER = tuple(2 * (SECOND[0] if s in SECOND[0] else SECOND[1]).index(s) + (s in SECOND[1]) for s in range(CROSS))
+LATER = tuple(29 - s if s in (14, 15) else 2 * (SECOND[0] if s in SECOND[0] else SECOND[1]).index(s) + (s in SECOND[1])
+              for s in range(CROSS))
 PAIRS = 33
 PARTS = (pl.ds(0, 256), pl.ds(256, 272))
 QUARTERS = (pl.ds(0, 128), pl.ds(128, 128), pl.ds(256, 128), pl.ds(384, 144))
@@ -112,8 +113,8 @@
         diag = s == 0
         k0 = jnp.where(diag, 0, jnp.where(below, k_low, 0))
         k1 = jnp.where(diag, 1, jnp.where(below, k_low, 1))
-        q0 = jnp.where(diag, 0, jnp.where(below, 0, q_high))
-        q1 = jnp.where(diag, 1, jnp.where(below, 1, q_high))
+        q0 = jnp.where(diag, 0, jnp.where(below, 1 - q_high, q_high))
+        q1 = jnp.where(diag, 1, q_high)
         return described(k0, q0, b0, b1), described(k1, q1, b0, b1)
 
     def pair_across():
@@ -220,11 +221,60 @@
             arrive(11)
             arrive(15)
 
-        @pl.when(i == 7)
-        def _():
+        scores_of(work, [(one, one, pairs(one)), (two, two, pairs(two))])
+        return 0
+
+    def into(q, was, more, op):
+        if q is None:
+            return [was[0], op(was[1], more)]
+        high = q == q_high
+        return [take(high, was[0], op(was[0], more)), take(high, op(was[1], more), was[1])]
+
+    def merge(units, fresh, c, _):
+        cols = pl.ds(pl.multiple_of(c * 256, 256), 256)
+        if fresh:
+            old = [jnp.full((8, 256), NEG, F32)] * 2
+            mass = weighted = [jnp.zeros((8, 256), F32)] * 2
+        else:
+            old, mass, weighted = ([total[2 * n + half, :, cols] for half in range(2)] for n in range(3))
+        tops = old
+        for n, q in units:
+            mine = stat[n, 0, :, cols]
+            tops = into(q, tops, mine, jnp.maximum)
+        if not fresh:
+            tops = [jnp.broadcast_to(jnp.max(top, axis=0, keepdims=True), (8, 256)) for top in tops]
+            keep = [jnp.exp2(was - top) for was, top in zip(old, tops)]
+            mass = [was * factor for was, factor in zip(mass, keep)]
+            weighted = [was * factor for was, factor in zip(weighted, keep)]
+        for n, q in units:
+            factor = jnp.exp2(stat[n, 0, :, cols] - (tops[1] if q is None else take(q == q_high, tops[1], tops[0])))
+            mass = into(q, mass, factor * stat[n, 1, :, cols], jnp.add)
+            weighted = into(q, weighted, factor * stat[n, 2, :, cols], jnp.add)
+        for half in range(2):
+            total[half, :, cols] = tops[half]
+            if fresh:
+                total[2 + half, :, cols] = mass[half]
+                total[4 + half, :, cols] = weighted[half]
+            else:
+                inverse = 1.0 / jnp.broadcast_to(jnp.sum(mass[half], axis=0, keepdims=True), (8, 256))
+                total[2 + half, :, cols] = inverse
+                total[4 + half, :, cols] = inverse * jnp.broadcast_to(
+                    jnp.sum(weighted[half], axis=0, keepdims=True), (8, 256))
+        return 0
+
+    def units_of(steps):
+        return [(2 * s + u, q if s == 0 or u == 0 else None) for s in steps for u, (_, q, _, _) in enumerate(pairs(s))]
+
+    def first_last(work, i, _):
+        s = 12 + i
+
+        @pl.when(i == 1)
+        def _():
+            seen = units_of([s for s in range(CROSS) if s != 13]) + [(2 * CROSS, None)]
+            lax.fori_loop(0, 4, functools.partial(merge, seen, True), 0)
             arrive(13)
 
-        scores_of(work, [(one, one, pairs(one)), (two, two, pairs(two))])
+        scores_of(work, [(s, s, pairs(s))])
         return 0
 
     def first(q_in, o_in, qct, oct_, raw_s, raw_g):
@@ -265,36 +315,13 @@
 
         work = (qct, oct_, raw_s, raw_g)
         scores_of(work, [(CROSS, 0, pair_across())])
-        lax.fori_loop(0, 8, functools.partial(first_pass, work), 0)
+        lax.fori_loop(0, 7, functools.partial(first_pass, work), 0)
+        lax.fori_loop(0, 2, functools.partial(first_last, work), 0)
 
     turned, raw = pltpu.VMEM((2 * SPAN, WIDE), BF16), pltpu.VMEM((4, 512, 256), F32)
     pl.run_scoped(first, turned, turned, turned, turned, raw, raw)
 
-    queries_of = [q for s in range(CROSS) for _, q, _, _ in pairs(s)] + [q_high]
-
-    def combine(c, _):
-        cols = pl.ds(pl.multiple_of(c * 256, 256), 256)
-        tops = [jnp.full((8, 256), NEG, F32)] * 2
-        for n, q in enumerate(queries_of):
-            mine = stat[n, 0, :, cols]
-            tops = [take(q == half, jnp.maximum(top, mine), top) for half, top in enumerate(tops)]
-        tops = [jnp.broadcast_to(jnp.max(top, axis=0, keepdims=True), (8, 256)) for top in tops]
-        mass = [jnp.zeros((8, 256), F32)] * 2
-        weighted = [jnp.zeros((8, 256), F32)] * 2
-        for n, q in enumerate(queries_of):
-            factor = jnp.exp2(stat[n, 0, :, cols] - take(q == 0, tops[0], tops[1]))
-            stat[n, 0, :, cols] = factor
-            more = factor * stat[n, 1, :, cols]
-            mass = [take(q == half, was + more, was) for half, was in enumerate(mass)]
-            more = factor * stat[n, 2, :, cols]
-            weighted = [take(q == half, was + more, was) for half, was in enumerate(weighted)]
-        for half in range(2):
-            inverse = 1.0 / jnp.broadcast_to(jnp.sum(mass[half], axis=0, keepdims=True), (8, 256))
-            total[half, :, cols] = inverse
-            total[2 + half, :, cols] = inverse * jnp.broadcast_to(jnp.sum(weighted[half], axis=0, keepdims=True), (8, 256))
-        return 0
-
-    lax.fori_loop(0, 4, combine, 0)
+    lax.fori_loop(0, 4, functools.partial(merge, units_of([13]), False), 0)
 
     def rows_of(part):
         return slice(part * SPAN, (part + 1) * SPAN)
@@ -327,14 +354,15 @@
         todo = []
         for s, units in group:
             for u, (k, q, least, _) in enumerate(units):
-                todo.append((2 * s + u, q == 0))
+                todo.append((2 * s + u, q != q_high))
         height = len(todo) * SPAN
         gate_acc = [jnp.zeros((SPAN, SPAN), F32) for _ in todo]
         for c in range(4):
             cols = slice(c * 256, (c + 1) * 256)
             for at, (n, first) in enumerate(todo):
-                factor = stat[n, 0, :, cols] * take(first, total[0, :, cols], total[1, :, cols])
-                delta = take(first, total[2, :, cols], total[3, :, cols])
+                factor = jnp.exp2(stat[n, 0, :, cols] - take(first, total[0, :, cols], total[1, :, cols]))
+                factor = factor * take(first, total[2, :, cols], total[3, :, cols])
+                delta = take(first, total[4, :, cols], total[5, :, cols])
                 prob = e_all[n, :, cols] * jnp.concatenate([factor] * 16, axis=0)
                 grad = prob * (p_all[n, :, cols] - jnp.concatenate([delta] * 16, axis=0))
                 gate_acc[at] = gate_acc[at] + grad[:, 0:128] + grad[:, 128:256]
@@ -380,49 +408,61 @@
         one, two = table(SECOND[0], i), table(SECOND[1], i)
         gradients_of(prob_low, grad_low, ds_all, i * 512, [(one, pairs(one)), (two, pairs(two))])
 
-        @pl.when(i <= 6)
-        def _():
-            to_partner(lax.div(two, 2), 1)
-
         @pl.when(i == 0)
         def _():
-            to_partner(lax.div(one, 2), 0)
-
-        @pl.when(i >= 1)
-        def _():
-            from_partner(lax.div(one, 2), 0)
-
-        @pl.when(i == 6)
-        def _():
-            join(2, (2, 3), (6,))
-
-        for at in range(1, CHIPS):
-            @pl.when(one == 2 * at)
+            to_partner(6, 0)
+            to_partner(5, 1)
+
+        @pl.when(i == 1)
+        def _():
+            for j, n in ((6, 0), (5, 1)):
+                from_partner(j, n)
+                for part in range(4):
+                    leave(j, part, cur.at[n], cur_gate.at[n])
+
+        @pl.when(i <= 1)
+        def _():
+            s = 15 - i
+            gradients_of(prob_low, grad_low, ds_all, 14 * 256 + i * 256, [(s, pairs(s))])
+
+            @pl.when(i == 0)
             def _():
+                to_partner(7, 0)
+
+            @pl.when(i == 1)
+            def _():
+                from_partner(7, 0)
                 for part in range(4):
-                    if at in (5, 6, 7) or (at, part // 2) in ((1, 1), (3, 0)):
-                        leave(at, part, cur.at[0], cur_gate.at[0])
-                if at in (1, 2, 3, 4):
-                    held[at - 1] = cur[0]
-                    held_gate[at - 1] = cur_gate[0]
-
-        @pl.when(i == 5)
-        def _():
-            join(2, (0, 1), (6,))
-
-        @pl.when(i == 7)
-        def _():
-            own[...] = cur[1]
-            own_gate[...] = cur_gate[1]
+                    leave(7, part, cur.at[0], cur_gate.at[0])
+
+        @pl.when(i == 2)
+        def _():
+            to_partner(2, 0)
+            to_partner(4, 1)
+
+        for at, j, mine in ((3, 1, 2), (4, 3, 4), (5, 0, 1), (6, None, 3)):
+            @pl.when(i == at)
+            def _():
+                if j is not None:
+                    to_partner(j, 1)
+                if at == 5:
+                    join(2, (2, 3), (6,))
+                from_partner(mine, 0)
+                for part in range(4):
+                    if (mine, part // 2) in ((1, 1), (3, 0)):
+                        leave(mine, part, cur.at[0], cur_gate.at[0])
+                held[mine - 1] = cur[0]
+                held_gate[mine - 1] = cur_gate[0]
+                if at == 4:
+                    join(2, (0, 1), (6,))
+                if at == 6:
+                    own[...] = cur[1]
+                    own_gate[...] = cur_gate[1]
 
         return 0
 
     def query_pass(ds_all, c, _):
         @pl.when(c == 1)
-        def _():
-            join(4, (2, 3), (5, 7))
-
-        @pl.when(c == 2)
         def _():
             join(1, (0, 1), (2,))
             join(3, (2, 3), (2,))
@@ -437,11 +477,11 @@
         return 0
 
     def second(prob_low, grad_low, ds_all):
-        lax.fori_loop(0, 8, functools.partial(second_pass, prob_low, grad_low, ds_all), 0)
+        lax.fori_loop(0, 7, functools.partial(second_pass, prob_low, grad_low, ds_all), 0)
         gradients_of(prob_low, grad_low, ds_all, CROSS * 256, [(CROSS, pair_across())])
         own[...] = own[...] + cur[0]
         own_gate[...] = own_gate[...] + cur_gate[0]
-        join(4, (0, 1), (5, 7))
+        join(4, (0, 1, 2, 3), (5, 7))
         lax.fori_loop(0, 4, functools.partial(query_pass, ds_all), 0)
 
     pl.run_scoped(second, pltpu.VMEM((512, WIDE), BF16), pltpu.VMEM((512, WIDE), BF16), pltpu.VMEM((PAIRS * SPAN, WIDE), BF16))
@@ -496,7 +536,7 @@
             pltpu.VMEM((PAIRS, SPAN, WIDE), F32),
             pltpu.VMEM((PAIRS, SPAN, WIDE), F32),
             pltpu.VMEM((PAIRS, 3, 8, WIDE), F32),
-            pltpu.VMEM((4, 8, WIDE), F32),
+            pltpu.VMEM((6, 8, WIDE), F32),
             pltpu.VMEM((2, 2 * rows, SPAN), F32),
             pltpu.VMEM((2, 8, SPAN), F32),
             pltpu.VMEM((2 * rows, SPAN), F32),

time: 35.8 us -> 35.3 us (0.986)
  Pallas kernels: 35 us -> 34.5 us
    pallas_call x1, Pallas kernels: 34.2 us -> 33.7 us  [on_device(): pl.pallas_call(kernel, out_shape=tuple((pltpu.VMEM(out.shape, out.dtype)...]
where the time goes in v4:
time: 35.3 us; the launch traced here: 35.2 us
  Pallas kernels  34.5 us (98%)
  between operations  0.64 us (2%)
    pallas_call x1, Pallas kernels, on_device(): pl.pallas_call(kernel, out_shape=tuple((pltpu.VMEM(out.shape, out.dtype)...  33.7 us
    pallas_call x1, Pallas kernels, on_device(): pl.pallas_call(hand_over, out_shape=outs, in_specs=[vmem] * 4, out_specs=...  0.86 us

profile of v4, /device:TPU:0, one launch (start us, length us, event | category | flops | bytes accessed | tf_op | source)
XLA Modules:
  0.0 35.2 jit_solution(14288618309474562651)
XLA Ops:
  0.6 33.7 %shard_map.93 = (bf16[256,1024]{1,0:T(8,128)(2,1)S(1)}, bf16[256,128]{1,0:T(8,128)(2,1)S(1)}, bf16[256,128]{1,0:T(8,128)(2,1)S(1)}, f32[1,256]{1,0:T(1,128)S(1)}) custom-call(s32[32]{0:T(128)} %place.1, bf16[256,1024]{1,0:T(8,128)(2,1)} %q_ref.1, bf16[256,128]{1,0:T(8,128)(2,1)} %k_ref.1, bf16[256,128]{1,0:T(8,128)(2,1)} %v_ref.1, bf16[1,256]{1,0:T(2,128)(2,1)} %bitcast.2, ...), custom_call_target="tpu_custom_call" | custom-call | tf_op jit(solution)/shard_map/pallas_call | solution.py:526
  34.3 0.9 %shard_map.94 = (bf16[256,1024]{1,0:T(8,128)(2,1)}, bf16[256,128]{1,0:T(8,128)(2,1)}, bf16[256,128]{1,0:T(8,128)(2,1)}, f32[1,256]{1,0:T(1,128)}) custom-call(bf16[256,1024]{1,0:T(8,128)(2,1)S(1)} %get-tuple-element.12.refs_0_, bf16[256,128]{1,0:T(8,128)(2,1)S(1)} %get-tuple-element.13.refs_1_, bf16[256,128]{1,0:T(8,128)(2,1)S(1)} %get-tuple-element.14.refs_2_, ...), custom_call_target="tpu_custom_call" | custom-call | tf_op jit(solution)/shard_map/pallas_call | solution.py:555

commit v5 on v4

--- a/solution.py
+++ b/solution.py
@@ -75,6 +75,12 @@
         pltpu.make_async_remote_copy(
             src_ref=where, dst_ref=where, send_sem=block_send, recv_sem=recv_sem(slot, part or 0),
             device_id={"ctx": partner}, device_id_type=MESH).wait_recv()
+
+    def quarter_copy(source, slot, quarter, target):
+        sem = {(2, 0): 2, (2, 1): 21, (6, 2): 19, (6, 3): 22, (4, 0): 4, (4, 1): 23, (4, 2): 18, (4, 3): 24}
+        return pltpu.make_async_remote_copy(
+            src_ref=blocks.at[source, QUARTERS[quarter]], dst_ref=blocks.at[slot, QUARTERS[quarter]], send_sem=block_send,
+            recv_sem=block_recv.at[sem.get((slot, quarter), slot)], device_id={"ctx": target}, device_id_type=MESH)
 
     def pass_on(slot):
         for part in range(2):
@@ -177,10 +183,11 @@
 
         @pl.when(i == 1)
         def _():
-            arrive(2, 0)
-            send(2, 4, 0, right)
-            arrive(6, 1)
-            send(6, 4, 1, left)
+            for quarter in (0, 1):
+                quarter_copy(2, 2, quarter, partner).wait_recv()
+                quarter_copy(2, 4, quarter, right).start()
+                quarter_copy(6, 6, quarter + 2, partner).wait_recv()
+                quarter_copy(6, 4, quarter + 2, left).start()
             for part in range(2):
                 arrive(8, part)
                 send(8, 10, part, right)
@@ -194,12 +201,15 @@
         @pl.when(i == 2)
         def _():
             arrive(3)
+            for quarter in (0, 2):
+                quarter_copy(4, 4, quarter, partner).wait_recv()
+                quarter_copy(4, 12, quarter, across).start()
 
         @pl.when(i == 3)
         def _():
-            for part in range(2):
-                arrive(4, part)
-                send(4, 12, part, across)
+            for quarter in (1, 3):
+                quarter_copy(4, 4, quarter, partner).wait_recv()
+                quarter_copy(4, 12, quarter, across).start()
             pass_on(4)
             arrive(7)
             arrive(9)
@@ -292,10 +302,12 @@
         pl.semaphore_wait(barrier, 4)
 
         loads[0].wait()
-        send(0, 2, 0, right)
+        for quarter in (0, 1):
+            quarter_copy(0, 2, quarter, right).start()
         send(0, 8, 0, across)
         loads[1].wait()
-        send(0, 6, 1, left)
+        for quarter in (2, 3):
+            quarter_copy(0, 6, quarter, left).start()
         send(0, 2, 1, right)
         send(0, 8, 1, across)
         send(0, 6, 0, left)
@@ -547,7 +559,7 @@
             pltpu.VMEM((CHIPS, ROWS, SPAN), BF16),
             pltpu.VMEM((CHIPS - 1, ROWS, SPAN), BF16),
             pltpu.VMEM((CHIPS - 1, ROWS, SPAN), BF16),
-            dma((4,)), dma, dma((21,)), dma, dma((CHIPS,)), dma, dma((CHIPS - 1, 4)),
+            dma((4,)), dma, dma((25,)), dma, dma((CHIPS,)), dma, dma((CHIPS - 1, 4)),
         ],
         compiler_params=pltpu.CompilerParams(
             collective_id=0, has_side_effects=True, vmem_limit_bytes=63 * 1024 * 1024),

time: 35.3 us -> 34.8 us (0.986)
  Pallas kernels: 34.5 us -> 34 us
    pallas_call x1, Pallas kernels: 33.7 us -> 33.2 us  [on_device(): pl.pallas_call(kernel, out_shape=tuple((pltpu.VMEM(out.shape, out.dtype)...]
where the time goes in v5:
time: 34.8 us; the launch traced here: 34.7 us
  Pallas kernels  34 us (98%)
  between operations  0.64 us (2%)
    pallas_call x1, Pallas kernels, on_device(): pl.pallas_call(kernel, out_shape=tuple((pltpu.VMEM(out.shape, out.dtype)...  33.2 us
    pallas_call x1, Pallas kernels, on_device(): pl.pallas_call(hand_over, out_shape=outs, in_specs=[vmem] * 4, out_specs=...  0.86 us

profile of v5, /device:TPU:0, one launch (start us, length us, event | category | flops | bytes accessed | tf_op | source)
XLA Modules:
  0.0 34.7 jit_solution(17699591957399619259)
XLA Ops:
  0.6 33.2 %shard_map.93 = (bf16[256,1024]{1,0:T(8,128)(2,1)S(1)}, bf16[256,128]{1,0:T(8,128)(2,1)S(1)}, bf16[256,128]{1,0:T(8,128)(2,1)S(1)}, f32[1,256]{1,0:T(1,128)S(1)}) custom-call(s32[32]{0:T(128)} %place.1, bf16[256,1024]{1,0:T(8,128)(2,1)} %q_ref.1, bf16[256,128]{1,0:T(8,128)(2,1)} %k_ref.1, bf16[256,128]{1,0:T(8,128)(2,1)} %v_ref.1, bf16[1,256]{1,0:T(2,128)(2,1)} %bitcast.2, ...), custom_call_target="tpu_custom_call" | custom-call | tf_op jit(solution)/shard_map/pallas_call | solution.py:538
  33.8 0.9 %shard_map.94 = (bf16[256,1024]{1,0:T(8,128)(2,1)}, bf16[256,128]{1,0:T(8,128)(2,1)}, bf16[256,128]{1,0:T(8,128)(2,1)}, f32[1,256]{1,0:T(1,128)}) custom-call(bf16[256,1024]{1,0:T(8,128)(2,1)S(1)} %get-tuple-element.12.refs_0_, bf16[256,128]{1,0:T(8,128)(2,1)S(1)} %get-tuple-element.13.refs_1_, bf16[256,128]{1,0:T(8,128)(2,1)S(1)} %get-tuple-element.14.refs_2_, ...), custom_call_target="tpu_custom_call" | custom-call | tf_op jit(solution)/shard_map/pallas_call | solution.py:567
